TPU v7x, 32 devices: a whole 2x2x4 slice. The times are simulated.
32 devices in a mesh: grp: 2 (over y), lon: 4 (over z), lat: 2 (over x), ch: 2 (over core).
Axes of the slice: x: 2, y: 2, z: 4, core: 2. Of those that a mesh axis runs over, the one named last changes fastest.
Arguments:
- features: bfloat16 [96, 256, 256], P(('grp', 'lat'), 'lon', 'ch'), parts along dimension 0, may hold values from -6 to 6
- dilation_rates: int32 [5], replicated, may hold values from 1 to 21, as said below
- branch_weight: bfloat16 [5, 3, 3, 256, 256], P(None, None, None, None, 'ch'), may hold values from -0.125 to 0.125
- branch_bias: float32 [5, 256], P(None, 'ch'), may hold values from -3 to 3
- merge_weight: bfloat16 [5, 256, 256], P(None, 'ch'), may hold values from -0.15625 to 0.15625
- cotangent: bfloat16 [96, 256, 256], P(('grp', 'lat'), 'lon', 'ch'), parts along dimension 0, may hold values from -6 to 6
Outputs:
- merged_out: bfloat16 [96, 256, 256], P(('grp', 'lat'), 'lon', 'ch'), parts along dimension 0
- feature_grad: bfloat16 [96, 256, 256], P(('grp', 'lat'), 'lon', 'ch'), parts along dimension 0
There are 2 independent parts, one for each index of `grp`. A program takes and returns all parts, laid end to end along the dimension named above; an argument that names none is the same for every part. Nothing has to cross between parts.
Inputs may be any that keep to these rules, and one draw needn't show every extreme that they name: `dilation_rates`: one branch has rate exactly 21.
All inputs are finite; a program needn't handle non-finite values.
Results may differ from a plain program's by a relative error of at most 0.005.
Values may be sent and summed in bfloat16 or wider, within the bound.
A program may use at most 192 MiB of HBM per device.

v0:
```python
import jax
import jax.numpy as jnp
from jax import lax
from jax.sharding import PartitionSpec as P

BRANCHES = 5
RMAX = 21


def with_halo(cells, sides, width, closed):
    for axis, dim in sides:
        count = lax.axis_size(axis)
        ends = count if closed else count - 1
        head = lax.slice_in_dim(cells, 0, width, axis=dim)
        tail = lax.slice_in_dim(cells, cells.shape[dim] - width, cells.shape[dim], axis=dim)
        cells = jnp.concatenate(
            [
                lax.ppermute(tail, axis, [(i, (i + 1) % count) for i in range(ends)]),
                cells,
                lax.ppermute(head, axis, [((i + 1) % count, i) for i in range(ends)]),
            ],
            axis=dim,
        )
    return cells


def silu_grad(preact):
    sigma = jax.nn.sigmoid(preact)
    return sigma * (1.0 + preact * (1.0 - sigma))


def on_device(features, dilation_rates, branch_weight, branch_bias, merge_weight, cotangent):
    lat_rows, lon_cols, half_channels = features.shape
    channels = merge_weight.shape[2]
    own_out = branch_weight.shape[4]
    cells = lat_rows * lon_cols
    reach = RMAX
    full_feat = lax.all_gather(features, "ch", axis=2, tiled=True)
    wide_lon = with_halo(full_feat, (("lon", 1),), reach, True)
    padded = with_halo(wide_lon, (("lat", 0),), reach, False)
    merged_total = jnp.zeros((cells, channels), jnp.float32)
    preacts = []
    for b in range(BRANCHES):
        spacing = dilation_rates[b]
        pieces = []
        for i in range(3):
            for j in range(3):
                pieces.append(
                    lax.dynamic_slice(
                        padded,
                        (reach + spacing * (i - 1), reach + spacing * (j - 1), 0),
                        (lat_rows, lon_cols, channels),
                    )
                )
        patches = jnp.concatenate(pieces, axis=2).reshape(cells, 9 * channels)
        preact = (
            jnp.dot(
                patches,
                branch_weight[b].reshape(9 * channels, own_out),
                preferred_element_type=jnp.float32,
            )
            + branch_bias[b]
        )
        activated = jax.nn.silu(preact).astype(jnp.bfloat16)
        merged_total = merged_total + jnp.dot(
            activated, merge_weight[b], preferred_element_type=jnp.float32
        )
        preacts.append(preact)
    merged_out = lax.psum_scatter(
        merged_total.reshape(lat_rows, lon_cols, channels), "ch", scatter_dimension=2, tiled=True
    ).astype(jnp.bfloat16)
    full_cot = lax.all_gather(cotangent, "ch", axis=2, tiled=True).reshape(cells, channels)
    grads = []
    for b in range(BRANCHES):
        dact = jnp.dot(full_cot, merge_weight[b].T, preferred_element_type=jnp.float32)
        grads.append((dact * silu_grad(preacts[b])).astype(jnp.bfloat16))
    branch_grads = jnp.concatenate(grads, axis=1).reshape(lat_rows, lon_cols, BRANCHES * own_out)
    grad_lon = with_halo(branch_grads, (("lon", 1),), reach, True)
    grad_pad = with_halo(grad_lon, (("lat", 0),), reach, False)
    partial_grad = jnp.zeros((cells, channels), jnp.float32)
    for b in range(BRANCHES):
        spacing = dilation_rates[b]
        pieces = []
        for i in range(3):
            for j in range(3):
                pieces.append(
                    lax.dynamic_slice(
                        grad_pad,
                        (reach - spacing * (i - 1), reach - spacing * (j - 1), b * own_out),
                        (lat_rows, lon_cols, own_out),
                    )
                )
        patches = jnp.concatenate(pieces, axis=2).reshape(cells, 9 * own_out)
        flipped = jnp.transpose(branch_weight[b], (0, 1, 3, 2)).reshape(9 * own_out, channels)
        partial_grad = partial_grad + jnp.dot(patches, flipped, preferred_element_type=jnp.float32)
    partial_grad = partial_grad.reshape(lat_rows, lon_cols, channels)
    feature_grad = lax.psum_scatter(partial_grad, "ch", scatter_dimension=2, tiled=True).astype(
        jnp.bfloat16
    )
    return (merged_out, feature_grad)


def solution(mesh):
    return jax.shard_map(
        on_device,
        mesh=mesh,
        in_specs=(
            P(("grp", "lat"), "lon", "ch"),
            P(),
            P(None, None, None, None, "ch"),
            P(None, "ch"),
            P(None, "ch", None),
            P(("grp", "lat"), "lon", "ch"),
        ),
        out_specs=(P(("grp", "lat"), "lon", "ch"), P(("grp", "lat"), "lon", "ch")),
        check_vma=False,
    )
```

profile of v0, /device:TPU:0, one launch (start us, length us, event | category | flops | bytes accessed | tf_op | source)
XLA Modules:
  0.0 271.9 jit_solution(14359448014499265545)
XLA Ops:
  10.0 3.0 %collective-permute-start = (bf16[24,21,256]{2,1,0:T(8,128)(2,1)S(1)}, bf16[24,21,256]{2,1,0:T(8,128)(2,1)S(1)}, u32[]{:S(2)}, u32[]{:S(2)}) collective-permute-start(bf16[24,21,256]{2,1,0:T(8,128)(2,1)S(1)} %get-tuple-element.108), channel_id=1, source_target_pairs={{0,4},{4,8},{8,12},{12,0},{1,5},{5,9},{9,13},{13,1},{2,6},{6,10},{... | collective-permute-start | bytes 774152 | tf_op jit(solution)/shard_map/ppermute | solution.py:18
  15.1 7.8 %collective-permute-done = bf16[24,21,256]{2,1,0:T(8,128)(2,1)S(1)} collective-permute-done((bf16[24,21,256]{2,1,0:T(8,128)(2,1)S(1)}, bf16[24,21,256]{2,1,0:T(8,128)(2,1)S(1)}, u32[]{:S(2)}, u32[]{:S(2)}) %collective-permute-start) | collective-permute-done | bytes 258080 | tf_op jit(solution)/shard_map/ppermute | solution.py:18
  22.8 5.2 %collective-permute-done.1 = bf16[24,21,256]{2,1,0:T(8,128)(2,1)S(1)} collective-permute-done((bf16[24,21,256]{2,1,0:T(8,128)(2,1)S(1)}, bf16[24,21,256]{2,1,0:T(8,128)(2,1)S(1)}, u32[]{:S(2)}, u32[]{:S(2)}) %collective-permute-start.1) | collective-permute-done | bytes 258080 | tf_op jit(solution)/shard_map/ppermute | solution.py:20
  31.0 4.4 %collective-permute-start.2 = (bf16[21,106,256]{2,1,0:T(8,128)(2,1)}, bf16[21,106,256]{2,1,0:T(8,128)(2,1)}, u32[]{:S(2)}, u32[]{:S(2)}) collective-permute-start(bf16[21,106,256]{2,1,0:T(8,128)(2,1)} %get-tuple-element.101), channel_id=1, source_target_pairs={{0,2},{1,3},{4,6},{5,7},{8,10},{9,11},{12,14},{13,15},{16,18},{17,... | collective-permute-start | bytes 3419144 | tf_op jit(solution)/shard_map/ppermute | solution.py:18
  52.6 4.6 %slice_bitcast_fusion.5 = (bf16[3,3,128,256]{2,3,1,0:T(8,128)(2,1)}, bf16[3,3,128,256]{2,3,1,0:T(8,128)(2,1)}, bf16[3,3,128,256]{2,3,1,0:T(8,128)(2,1)}, bf16[3,...) fusion(bf16[5,3,3,256,128]{4,3,2,1,0:T(8,128)(2,1)} %param.8), kind=kLoop, calls=%fused_computation.168 | loop fusion | bytes 8847360 | tf_op jit(solution)/shard_map/transpose | solution.py:94
  57.2 2.9 %collective-permute-done.2 = bf16[21,106,256]{2,1,0:T(8,128)(2,1)} collective-permute-done((bf16[21,106,256]{2,1,0:T(8,128)(2,1)}, bf16[21,106,256]{2,1,0:T(8,128)(2,1)}, u32[]{:S(2)}, u32[]{:S(2)}) %collective-permute-start.2) | collective-permute-done | bytes 1139744 | tf_op jit(solution)/shard_map/ppermute | solution.py:18
  60.1 5.2 %collective-permute-done.3 = bf16[21,106,256]{2,1,0:T(8,128)(2,1)} collective-permute-done((bf16[21,106,256]{2,1,0:T(8,128)(2,1)}, bf16[21,106,256]{2,1,0:T(8,128)(2,1)}, u32[]{:S(2)}, u32[]{:S(2)}) %collective-permute-start.3) | collective-permute-done | bytes 1139744 | tf_op jit(solution)/shard_map/ppermute | solution.py:20
  70.3 3.5 %dynamic-slice_dynamic-update-slice_fusion.6 = (bf16[24,64,2304]{2,1,0:T(8,128)(2,1)S(1)}, bf16[24,64,2304]{2,1,0:T(8,128)(2,1)S(1)}, bf16[24,64,2304]{2,1,0:T(8...) fusion(bf16[24,64,2304]{2,1,0:T(8,128)(2,1)S(1)} %get-tuple-element.77, ...), kind=kLoop, calls=%fused_computation.40 | loop fusion | bytes 7864340
  73.8 3.6 %dynamic-slice_dynamic-update-slice_fusion.5 = (bf16[24,64,2304]{2,1,0:T(8,128)(2,1)S(1)}, bf16[24,64,2304]{2,1,0:T(8,128)(2,1)S(1)}, bf16[24,64,2304]{2,1,0:T(8...) fusion(bf16[24,64,2304]{2,1,0:T(8,128)(2,1)S(1)} %get-tuple-element.72, ...), kind=kLoop, calls=%fused_computation.39 | loop fusion | bytes 7864360
  77.4 3.5 %dynamic-slice_dynamic-update-slice_fusion.4 = (bf16[24,64,2304]{2,1,0:T(8,128)(2,1)S(1)}, bf16[24,64,2304]{2,1,0:T(8,128)(2,1)S(1)}, bf16[24,64,2304]{2,1,0:T(8...) fusion(bf16[24,64,2304]{2,1,0:T(8,128)(2,1)S(1)} %get-tuple-element.67, ...), kind=kLoop, calls=%fused_computation.38 | loop fusion | bytes 7864340
  82.3 3.6 %dynamic-slice_dynamic-update-slice_fusion.3 = (bf16[24,64,2304]{2,1,0:T(8,128)(2,1)S(1)}, bf16[24,64,2304]{2,1,0:T(8,128)(2,1)S(1)}, bf16[24,64,2304]{2,1,0:T(8...) fusion(bf16[24,64,2304]{2,1,0:T(8,128)(2,1)S(1)} %get-tuple-element.103, ...), kind=kLoop, calls=%fused_computation.37 | loop fusion | bytes 7864340
  85.9 3.7 %dynamic-slice_dynamic-update-slice_fusion.2 = (bf16[24,64,2304]{2,1,0:T(8,128)(2,1)S(1)}, bf16[24,64,2304]{2,1,0:T(8,128)(2,1)S(1)}, bf16[24,64,2304]{2,1,0:T(8...) fusion(bf16[24,64,2304]{2,1,0:T(8,128)(2,1)S(1)} %get-tuple-element.57, ...), kind=kLoop, calls=%fused_computation.36 | loop fusion | bytes 7864360
  89.5 3.5 %dynamic-slice_dynamic-update-slice_fusion.1 = (bf16[24,64,2304]{2,1,0:T(8,128)(2,1)S(1)}, bf16[24,64,2304]{2,1,0:T(8,128)(2,1)S(1)}, bf16[24,64,2304]{2,1,0:T(8...) fusion(bf16[24,64,2304]{2,1,0:T(8,128)(2,1)S(1)} %get-tuple-element.52, ...), kind=kLoop, calls=%fused_computation.35 | loop fusion | bytes 7864340
  93.0 3.5 %dynamic-slice_dynamic-update-slice_fusion = (bf16[24,64,2304]{2,1,0:T(8,128)(2,1)S(1)}, bf16[24,64,2304]{2,1,0:T(8,128)(2,1)S(1)}, bf16[24,64,2304]{2,1,0:T(8,1...) fusion(bf16[24,64,2304]{2,1,0:T(8,128)(2,1)S(1)} %get-tuple-element.47, ...), kind=kLoop, calls=%fused_computation.34 | loop fusion | bytes 7864360 | tf_op jit(solution)/shard_map/concatenate | solution.py:55
  96.6 6.4 %convolution_add_fusion.12 = f32[1536,128]{0,1:T(8,128)} fusion(bf16[1536,2304]{1,0:T(8,128)(2,1)} %bitcast.172, bf16[2304,128]{1,0:T(8,128)(2,1)S(1)} %bitcast.182, f32[128]{0:T(128)S(1)} %get-tuple-element.113), kind=kOutput, calls=%fused_computation.20 | convolution fusion | flops 906166272 | bytes 8454656 | tf_op jit(solution)/shard_map/dot_general | solution.py:57
  123.0 2.8 %copy.20 = bf16[1536,640]{1,0:T(8,128)(2,1)S(1)} copy(bf16[1536,640]{0,1:T(8,128)(2,1)} %fusion.9) | data formatting | bytes 3932160 | tf_op jit(solution)/shard_map/concatenate | solution.py:77
  130.1 15.3 %collective-permute-done.4 = bf16[24,21,640]{2,0,1:T(8,128)(2,1)S(1)} collective-permute-done((bf16[24,21,640]{2,0,1:T(8,128)(2,1)S(1)}, bf16[24,21,640]{2,0,1:T(8,128)(2,1)S(1)}, u32[]{:S(2)}, u32[]{:S(2)}) %collective-permute-start.4) | collective-permute-done | bytes 645152 | tf_op jit(solution)/shard_map/ppermute | solution.py:18
  145.5 11.0 %collective-permute-done.5 = bf16[24,21,640]{2,0,1:T(8,128)(2,1)S(1)} collective-permute-done((bf16[24,21,640]{2,0,1:T(8,128)(2,1)S(1)}, bf16[24,21,640]{2,0,1:T(8,128)(2,1)S(1)}, u32[]{:S(2)}, u32[]{:S(2)}) %collective-permute-start.5) | collective-permute-done | bytes 645152 | tf_op jit(solution)/shard_map/ppermute | solution.py:20
  157.8 3.0 %fusion.41 = (bf16[21,106,640]{2,1,0:T(8,128)(2,1)}, bf16[21,106,640]{2,1,0:T(8,128)(2,1)}) fusion(bf16[24,106,640]{2,1,0:T(8,128)(2,1)S(1)} %pad_maximum_fusion.2), kind=kLoop, calls=%fused_computation.173 | loop fusion | bytes 11397120 | tf_op jit(solution)/shard_map/slice | solution.py:15
  160.7 3.1 %collective-permute-start.6 = (bf16[21,106,640]{2,1,0:T(8,128)(2,1)}, bf16[21,106,640]{2,1,0:T(8,128)(2,1)}, u32[]{:S(2)}, u32[]{:S(2)}) collective-permute-start(bf16[21,106,640]{2,1,0:T(8,128)(2,1)} %get-tuple-element.82), channel_id=1, source_target_pairs={{0,2},{1,3},{4,6},{5,7},{8,10},{9,11},{12,14},{13,15},{16,18},{17,... | collective-permute-start | bytes 8547848 | tf_op jit(solution)/shard_map/ppermute | solution.py:18
  190.3 36.9 %collective-permute-done.6 = bf16[21,106,640]{2,1,0:T(8,128)(2,1)} collective-permute-done((bf16[21,106,640]{2,1,0:T(8,128)(2,1)}, bf16[21,106,640]{2,1,0:T(8,128)(2,1)}, u32[]{:S(2)}, u32[]{:S(2)}) %collective-permute-start.6) | collective-permute-done | bytes 2849312 | tf_op jit(solution)/shard_map/ppermute | solution.py:18
  227.2 5.7 %collective-permute-done.7 = bf16[21,106,640]{2,1,0:T(8,128)(2,1)} collective-permute-done((bf16[21,106,640]{2,1,0:T(8,128)(2,1)}, bf16[21,106,640]{2,1,0:T(8,128)(2,1)}, u32[]{:S(2)}, u32[]{:S(2)}) %collective-permute-start.7) | collective-permute-done | bytes 2849312 | tf_op jit(solution)/shard_map/ppermute | solution.py:20
  232.9 5.5 %pad_maximum_fusion = bf16[66,106,640]{2,1,0:T(8,128)(2,1)S(1)} fusion(bf16[21,106,640]{2,1,0:T(8,128)(2,1)} %collective-permute-done.7, bf16[24,21,640]{2,1,0:T(8,128)(2,1)S(1)} %copy.24, bf16[24,64,640]{2,1,0:T(8,128)(2,1)S(1)} %bitcast.166, bf16[24,21,640]{2,1,0:T(8,128)(2,1)S(1)} %copy.23, bf16[21,106,640]{2,1,0:T(8,128)(2,1)} %collective-permute-done.6), kind=kLoop, calls=%fused_computation | loop fusion | flops 44774400 | bytes 17909760 | tf_op jit(solution)/shard_map/concatenate | solution.py:16
  258.4 4.5 %reduce-scatter.5.cloned.1.call-done = f32[24,64,128]{2,1,0:T(8,128)} async-done(((f32[24,64,256]{2,1,0:T(8,128)}), f32[24,64,128]{2,1,0:T(8,128)}) %reduce-scatter.5.cloned.1.call-update) | async-done | bytes 786448 | tf_op jit(solution)/shard_map/reduce_scatter | solution.py:97
  (105 shorter events, 83.0 us)
Async XLA Ops:
  7.2 249.3 %reduce-scatter.3.cloned.1.call-start = ((), (), s32[]{:S(2)}) async-start(), calls=%async_computation.2 | async-start | bytes 2359296 | tf_op jit(solution)/shard_map/reduce_scatter | solution.py:69
  10.0 12.9 %collective-permute-start = (bf16[24,21,256]{2,1,0:T(8,128)(2,1)S(1)}, bf16[24,21,256]{2,1,0:T(8,128)(2,1)S(1)}, u32[]{:S(2)}, u32[]{:S(2)}) collective-permute-start(bf16[24,21,256]{2,1,0:T(8,128)(2,1)S(1)} %get-tuple-element.108), channel_id=1, source_target_pairs={{0,4},{4,8},{8,12},{12,0},{1,5},{5,9},{9,13},{13,1},{2,6},{6,10},{... | collective-permute-start | bytes 774152 | tf_op jit(solution)/shard_map/ppermute | solution.py:18
  13.0 23.8 %copy-start.18 = (s32[5]{0:T(128)S(1)}, s32[5]{0:T(128)}, u32[]{:S(2)}) copy-start(s32[5]{0:T(128)} %param.7) | copy-start | bytes 64
  13.0 37.1 %copy-start.17 = (bf16[24,64,128]{2,1,0:T(8,128)(2,1)S(1)}, bf16[24,64,128]{2,1,0:T(8,128)(2,1)}, u32[]{:S(2)}) copy-start(bf16[24,64,128]{2,1,0:T(8,128)(2,1)} %param.11) | copy-start | bytes 1179652
  13.0 15.1 %collective-permute-start.1 = (bf16[24,21,256]{2,1,0:T(8,128)(2,1)S(1)}, bf16[24,21,256]{2,1,0:T(8,128)(2,1)S(1)}, u32[]{:S(2)}, u32[]{:S(2)}) collective-permute-start(bf16[24,21,256]{2,1,0:T(8,128)(2,1)S(1)} %get-tuple-element.109), channel_id=1, source_target_pairs={{4,0},{8,4},{12,8},{0,12},{5,1},{9,5},{13,9},{1,13},{6,2},{10,6},{... | collective-permute-start | bytes 774152 | tf_op jit(solution)/shard_map/ppermute | solution.py:20
  29.4 23.2 %copy-start.19 = (f32[5,128]{1,0:T(8,128)S(1)}, f32[5,128]{1,0:T(8,128)}, u32[]{:S(2)}) copy-start(f32[5,128]{1,0:T(8,128)} %param.9) | copy-start | bytes 7684
  31.0 29.0 %collective-permute-start.2 = (bf16[21,106,256]{2,1,0:T(8,128)(2,1)}, bf16[21,106,256]{2,1,0:T(8,128)(2,1)}, u32[]{:S(2)}, u32[]{:S(2)}) collective-permute-start(bf16[21,106,256]{2,1,0:T(8,128)(2,1)} %get-tuple-element.101), channel_id=1, source_target_pairs={{0,2},{1,3},{4,6},{5,7},{8,10},{9,11},{12,14},{13,15},{16,18},{17,... | collective-permute-start | bytes 3419144 | tf_op jit(solution)/shard_map/ppermute | solution.py:18
  35.4 29.8 %collective-permute-start.3 = (bf16[21,106,256]{2,1,0:T(8,128)(2,1)}, bf16[21,106,256]{2,1,0:T(8,128)(2,1)}, u32[]{:S(2)}, u32[]{:S(2)}) collective-permute-start(bf16[21,106,256]{2,1,0:T(8,128)(2,1)} %get-tuple-element.102), channel_id=1, source_target_pairs={{2,0},{3,1},{6,4},{7,5},{10,8},{11,9},{14,12},{15,13},{18,16},{19,... | collective-permute-start | bytes 3419144 | tf_op jit(solution)/shard_map/ppermute | solution.py:20
  52.6 12.6 %copy-start.14 = (bf16[24,21,256]{2,1,0:T(8,128)(2,1)S(1)}, bf16[24,21,256]{2,1,0:T(8,128)(2,1)}, u32[]{:S(2)}) copy-start(bf16[24,21,256]{2,1,0:T(8,128)(2,1)} %copy-done.13) | copy-start | bytes 774148
  93.0 3.6 %copy-start = (bf16[1,3,3,256,128]{4,3,2,1,0:T(8,128)(2,1)S(1)}, bf16[1,3,3,256,128]{4,3,2,1,0:T(8,128)(2,1)}, u32[]{:S(2)}) copy-start(bf16[1,3,3,256,128]{4,3,2,1,0:T(8,128)(2,1)} %get-tuple-element.91) | copy-start | bytes 1769476
  108.1 5.1 %copy-start.5 = (f32[1536,128]{0,1:T(8,128)}, f32[1536,128]{0,1:T(8,128)S(1)}, u32[]{:S(2)}) copy-start(f32[1536,128]{0,1:T(8,128)S(1)} %convolution_add_fusion.11) | copy-start | bytes 2359300
  110.7 2.5 copy-start.15
  110.8 2.5 copy-start.20
  113.2 3.9 %copy-start.7 = (f32[1536,128]{0,1:T(8,128)}, f32[1536,128]{0,1:T(8,128)S(1)}, u32[]{:S(2)}) copy-start(f32[1536,128]{0,1:T(8,128)S(1)} %convolution_add_fusion.10) | copy-start | bytes 2359300
  117.2 3.7 %copy-start.9 = (f32[1536,128]{0,1:T(8,128)}, f32[1536,128]{0,1:T(8,128)S(1)}, u32[]{:S(2)}) copy-start(f32[1536,128]{0,1:T(8,128)S(1)} %convolution_add_fusion.9) | copy-start | bytes 2359300
  126.1 19.3 %collective-permute-start.4 = (bf16[24,21,640]{2,0,1:T(8,128)(2,1)S(1)}, bf16[24,21,640]{2,0,1:T(8,128)(2,1)S(1)}, u32[]{:S(2)}, u32[]{:S(2)}) collective-permute-start(bf16[24,21,640]{2,0,1:T(8,128)(2,1)S(1)} %copy.21), channel_id=1, source_target_pairs={{0,4},{4,8},{8,12},{12,0},{1,5},{5,9},{9,13},{13,1},{2,6},{6,10},{... | collective-permute-start | bytes 1935368 | tf_op jit(solution)/shard_map/ppermute | solution.py:18
  127.9 28.5 %collective-permute-start.5 = (bf16[24,21,640]{2,0,1:T(8,128)(2,1)S(1)}, bf16[24,21,640]{2,0,1:T(8,128)(2,1)S(1)}, u32[]{:S(2)}, u32[]{:S(2)}) collective-permute-start(bf16[24,21,640]{2,0,1:T(8,128)(2,1)S(1)} %copy.22), channel_id=1, source_target_pairs={{4,0},{8,4},{12,8},{0,12},{5,1},{9,5},{13,9},{1,13},{6,2},{10,6},{... | collective-permute-start | bytes 1935368 | tf_op jit(solution)/shard_map/ppermute | solution.py:20
  160.7 66.5 %collective-permute-start.6 = (bf16[21,106,640]{2,1,0:T(8,128)(2,1)}, bf16[21,106,640]{2,1,0:T(8,128)(2,1)}, u32[]{:S(2)}, u32[]{:S(2)}) collective-permute-start(bf16[21,106,640]{2,1,0:T(8,128)(2,1)} %get-tuple-element.82), channel_id=1, source_target_pairs={{0,2},{1,3},{4,6},{5,7},{8,10},{9,11},{12,14},{13,15},{16,18},{17,... | collective-permute-start | bytes 8547848 | tf_op jit(solution)/shard_map/ppermute | solution.py:18
  163.8 69.1 %collective-permute-start.7 = (bf16[21,106,640]{2,1,0:T(8,128)(2,1)}, bf16[21,106,640]{2,1,0:T(8,128)(2,1)}, u32[]{:S(2)}, u32[]{:S(2)}) collective-permute-start(bf16[21,106,640]{2,1,0:T(8,128)(2,1)} %get-tuple-element.83), channel_id=1, source_target_pairs={{2,0},{3,1},{6,4},{7,5},{10,8},{11,9},{14,12},{15,13},{18,16},{19,... | collective-permute-start | bytes 8547848 | tf_op jit(solution)/shard_map/ppermute | solution.py:20
  185.3 1.7 copy-start.6
  185.3 1.7 copy-start.21
  185.3 2.2 copy-start.8
  190.3 72.7 %reduce-scatter.5.cloned.1.call-start = ((), (), s32[]{:S(2)}) async-start(), calls=%async_computation.3 | async-start | bytes 2359296 | tf_op jit(solution)/shard_map/reduce_scatter | solution.py:97
  246.4 2.5 copy-start.16
  (8 other events, 9.0 us)
Sparse Core Ops, SparseCore 0:
  190.4 11.7 reduce-scatter.2
  256.5 6.3 reduce-scatter.4
where the time goes:
time: 276 us; the launch traced here: 272 us
  waiting for transfers between devices  94.5 us (34%)
  local copies, waits for them, and re-layouts  64.9 us (24%)
  matrix products  37.5 us (14%)
  between operations  36.9 us (13%)
  starting transfers between devices  19.2 us (7%)
  other arithmetic  13.8 us (5%)
  blocking collectives  5.16 us (2%)
    ppermute x4, waiting for transfers between devices, with_halo(): lax.ppermute(tail, axis, [(i, (i + 1) % count) for i in range(ends)])  62.8 us
    unnamed x60, local copies, waits for them, and re-layouts  36.3 us
    ppermute x4, waiting for transfers between devices, with_halo(): lax.ppermute(head, axis, [((i + 1) % count, i) for i in range(ends)])  27.1 us
    dot_general x5, matrix products, on_device(): jnp.dot(patches, branch_weight[b].reshape(9 * channels, own_out), preferr...  16.4 us
    transpose x6, local copies, waits for them, and re-layouts, on_device(): jnp.transpose(branch_weight[b], (0, 1, 3, 2)).reshape(9 * own_out, channels)  15.2 us
    ppermute x4, starting transfers between devices, with_halo(): lax.ppermute(tail, axis, [(i, (i + 1) % count) for i in range(ends)])  12.3 us
    concatenate x4, other arithmetic, with_halo(): jnp.concatenate([lax.ppermute(tail, axis, [(i, (i + 1) % count) for i in...  9.9 us
    dot_general x5, matrix products, on_device(): jnp.dot(full_cot, merge_weight[b].T, preferred_element_type=jnp.float32)  9.02 us
  transfers between devices with their start and end apart: 10, of which 9 were waited for; matrix products, arithmetic and copies ran while one was open for 17% of the time, Pallas kernels for 0%

commit v1 on v0

v1 whole, which is shorter than its diff:
```python
import functools

import jax
import jax.numpy as jnp
from jax import lax
from jax.experimental import pallas as pl
from jax.experimental.pallas import tpu as pltpu
from jax.sharding import PartitionSpec as P

BRANCHES = 5
RMAX = 21
PADL = 24
LANES = 128
MESH = pl.DeviceIdType.MESH
ROW_CHUNK = 8

SIDES = ((-1, 0), (1, 0), (0, -1), (0, 1), (-1, -1), (-1, 1), (1, -1), (1, 1))


def opposite(k):
    return SIDES.index((-SIDES[k][0], -SIDES[k][1]))


def strip_rows(rows):
    return (rows * RMAX + 15) // 16 * 16


class Where:
    def __init__(self, n_lat, n_lon):
        self.grp = lax.axis_index("grp")
        self.lon = lax.axis_index("lon")
        self.lat = lax.axis_index("lat")
        self.ch = lax.axis_index("ch")
        self.n_lat, self.n_lon = n_lat, n_lon
        self.up = self.lat > 0
        self.down = self.lat < n_lat - 1

    def sibling(self):
        return (self.grp, self.lon, self.lat, 1 - self.ch)

    def side(self, k):
        dlat, dlon = SIDES[k]
        lon = lax.rem(self.lon + dlon + self.n_lon, self.n_lon) if dlon else self.lon
        return (self.grp, lon, self.lat + dlat, self.ch)

    def when(self, k, body):
        dlat = SIDES[k][0]
        if dlat == 0:
            body()
        else:
            pl.when(self.up if dlat < 0 else self.down)(body)

    def barrier(self):
        sem = pltpu.get_barrier_semaphore()
        pl.semaphore_signal(sem, inc=1, device_id=self.sibling(), device_id_type=MESH)
        for k in range(8):
            self.when(
                k,
                lambda k=k: pl.semaphore_signal(
                    sem, inc=1, device_id=self.side(k), device_id_type=MESH
                ),
            )
        pl.semaphore_wait(
            sem, 3 + 3 * self.up.astype(jnp.int32) + 3 * self.down.astype(jnp.int32)
        )


def gather_kernel(n_lat, n_lon, rows, feat, cot, left, right, *refs):
    pieces = refs[:8]
    full_feat, full_cot = refs[8:10]
    send, recv, send2, recv2, local = refs[10:]
    at = Where(n_lat, n_lon)
    me = at.ch
    at.barrier()

    def source(k):
        dlat, dlon = SIDES[k]
        if dlon < 0:
            return left
        if dlon > 0:
            return right
        return feat.at[pl.ds(0, RMAX)] if dlat < 0 else feat.at[pl.ds(rows - RMAX, RMAX)]

    def to_side(k):
        return pltpu.make_async_remote_copy(
            source(k),
            pieces[opposite(k)].at[me],
            send.at[k],
            recv.at[opposite(k)],
            device_id=at.side(k),
            device_id_type=MESH,
        )

    def forward(k):
        return pltpu.make_async_remote_copy(
            pieces[k].at[me],
            pieces[k].at[me],
            send2.at[k],
            recv2.at[k],
            device_id=at.sibling(),
            device_id_type=MESH,
        )

    order = (4, 5, 6, 7, 0, 1, 2, 3)
    for k in order:
        at.when(k, lambda k=k: to_side(k).start())
    own = []
    for n, (src, dst) in enumerate(((feat, full_feat), (cot, full_cot))):
        own.append(
            pltpu.make_async_remote_copy(
                src,
                dst.at[me],
                send2.at[8 + n],
                recv2.at[8 + n],
                device_id=at.sibling(),
                device_id_type=MESH,
            )
        )
        own[-1].start()
    copies = []
    for n, (src, dst) in enumerate(((feat, full_feat), (cot, full_cot))):
        copies.append(pltpu.make_async_copy(src, dst.at[me], local.at[n]))
        copies[-1].start()

    def arrive(k):
        pltpu.make_async_remote_copy(
            pieces[k].at[me],
            pieces[k].at[me],
            send.at[k],
            recv.at[k],
            device_id=at.sibling(),
            device_id_type=MESH,
        ).wait_recv()
        forward(k).start()

    for k in (2, 3, 0, 1, 4, 5, 6, 7):
        at.when(k, lambda k=k: arrive(k))

    def other_arrives(k):
        pltpu.make_async_remote_copy(
            pieces[k].at[1 - me],
            pieces[k].at[1 - me],
            send2.at[k],
            recv2.at[k],
            device_id=at.sibling(),
            device_id_type=MESH,
        ).wait_recv()
        forward(k).wait_send()
        to_side(k).wait_send()

    for k in range(8):
        at.when(k, lambda k=k: other_arrives(k))
    for n, dst in enumerate((full_feat, full_cot)):
        own[n].wait_send()
        pltpu.make_async_remote_copy(
            dst.at[1 - me],
            dst.at[1 - me],
            send2.at[8 + n],
            recv2.at[8 + n],
            device_id=at.sibling(),
            device_id_type=MESH,
        ).wait_recv()
        copies[n].wait()


def head_kernel(
    rows, cols, info, weight, bias, merge, feat, cot, p0, p1, p2, p3, p4, p5, p6, p7,
    m_out, c_out, g0, g1, g2, g3, g4, g5, g6, g7, padded, total, merged, strip,
):
    b = pl.program_id(0)
    pieces = (p0, p1, p2, p3, p4, p5, p6, p7)
    grads = (g0, g1, g2, g3, g4, g5, g6, g7)
    all_rows = rows + 2 * RMAX
    has_up, has_down = info[BRANCHES] > 0, info[BRANCHES + 1] > 0
    right_col = PADL + cols
    near = rows * RMAX

    @pl.when(b == 0)
    def _():
        for c in range(2):
            padded[c, RMAX : RMAX + rows, PADL:right_col, :] = feat[c].astype(jnp.float32)
            for k in range(8):
                dlat, dlon = SIDES[k]
                top = {-1: 0, 0: RMAX, 1: RMAX + rows}[dlat]
                count = rows if dlat == 0 else RMAX
                skip = rows - RMAX if dlat < 0 else 0
                if dlon == 0:
                    lo, hi = PADL, right_col
                elif dlon < 0:
                    lo, hi = PADL - RMAX, PADL
                else:
                    lo, hi = right_col, right_col + RMAX

                def fill(k=k, c=c, top=top, count=count, skip=skip, lo=lo, hi=hi, dlon=dlon):
                    if dlon == 0:
                        padded[c, top : top + count, lo:hi, :] = pieces[k][c].astype(jnp.float32)
                    else:
                        strip[...] = pieces[k][c].astype(jnp.float32)
                        for n in range(count):
                            start = (skip + n) * RMAX
                            padded[c, top + n, lo:hi, :] = strip[start : start + RMAX, :]

                if dlat == 0:
                    fill()
                else:
                    there = has_up if dlat < 0 else has_down
                    pl.when(there)(fill)

                    @pl.when(jnp.logical_not(there))
                    def _(c=c, top=top, count=count, lo=lo, hi=hi):
                        padded[c, top : top + count, lo:hi, :] = jnp.zeros(
                            (count, hi - lo, LANES), jnp.float32
                        )
        total[...] = jnp.zeros_like(total)
        merged[...] = jnp.zeros_like(merged)

    rate = info[b]
    cells = ROW_CHUNK * cols

    def chunk(n, _):
        row = n * ROW_CHUNK
        taps = []
        for i in range(3):
            for j in range(3):
                for c in range(2):
                    tap = padded[
                        c,
                        pl.ds(row + RMAX + rate * (i - 1), ROW_CHUNK),
                        pl.ds(PADL + rate * (j - 1), cols),
                        :,
                    ]
                    taps.append(tap.reshape(cells, LANES).astype(jnp.bfloat16))
        preact = jnp.dot(
            jnp.concatenate(taps, axis=1),
            weight[0].reshape(9 * 2 * LANES, LANES),
            preferred_element_type=jnp.float32,
        )
        preact = preact + bias[0]
        sigma = 1.0 / (1.0 + jnp.exp(-preact))
        activated = (preact * sigma).astype(jnp.bfloat16)
        here = pl.ds(pl.multiple_of(row * cols, cells), cells)
        merged[here, :] += jnp.dot(activated, merge[0], preferred_element_type=jnp.float32)
        own_cot = jnp.concatenate(
            [cot[c, pl.ds(row, ROW_CHUNK)].reshape(cells, LANES) for c in range(2)], axis=1
        )
        dact = lax.dot_general(
            own_cot, merge[0], (((1,), (1,)), ((), ())), preferred_element_type=jnp.float32
        )
        dpre = (dact * (sigma * (1.0 + preact * (1.0 - sigma)))).astype(jnp.bfloat16)
        for i in range(3):
            for j in range(3):
                part = lax.dot_general(
                    dpre,
                    weight[0, i, j],
                    (((1,), (1,)), ((), ())),
                    preferred_element_type=jnp.float32,
                )
                for c in range(2):
                    total[
                        c,
                        pl.ds(row + RMAX + rate * (i - 1), ROW_CHUNK),
                        pl.ds(PADL + rate * (j - 1), cols),
                        :,
                    ] += part[:, c * LANES : (c + 1) * LANES].reshape(ROW_CHUNK, cols, LANES)
        return 0

    lax.fori_loop(0, rows // ROW_CHUNK, chunk, 0)

    @pl.when(b == BRANCHES - 1)
    def _():
        for c in range(2):
            m_out[c] = (
                merged[:, c * LANES : (c + 1) * LANES]
                .astype(jnp.bfloat16)
                .reshape(rows, cols, LANES)
            )
            c_out[c] = total[c, RMAX : RMAX + rows, PADL:right_col, :].astype(jnp.bfloat16)
            for k in range(8):
                dlat, dlon = SIDES[k]
                top = {-1: 0, 0: RMAX, 1: RMAX + rows}[dlat]
                count = rows if dlat == 0 else RMAX
                skip = rows - RMAX if dlat < 0 else 0
                if dlon == 0:
                    grads[k][c] = total[c, top : top + count, PADL:right_col, :].astype(
                        jnp.bfloat16
                    )
                    continue
                lo = PADL - RMAX if dlon < 0 else right_col
                strip[...] = jnp.zeros_like(strip)
                for n in range(count):
                    start = (skip + n) * RMAX
                    strip[start : start + RMAX, :] = total[c, top + n, lo : lo + RMAX, :]
                grads[k][c] = strip[...].astype(jnp.bfloat16)


def scatter_kernel(n_lat, n_lon, rows, cols, m_part, c_part, *refs):
    parts = refs[:8]
    m_out, g_out = refs[8:10]
    from_sib = refs[10:18]
    staged = refs[18:26]
    landed = refs[26:34]
    m_sib, c_sib, acc, strip, send, recv, send2, recv2 = refs[34:]
    at = Where(n_lat, n_lon)
    me = at.ch
    at.barrier()

    def to_sibling(src, dst, n):
        return pltpu.make_async_remote_copy(
            src.at[1 - me], dst, send2.at[n], recv2.at[n],
            device_id=at.sibling(), device_id_type=MESH,
        )

    def to_side(k):
        return pltpu.make_async_remote_copy(
            staged[k], landed[opposite(k)], send.at[k], recv.at[opposite(k)],
            device_id=at.side(k), device_id_type=MESH,
        )

    order = (4, 5, 6, 7, 0, 1, 2, 3)
    for k in order:
        at.when(k, lambda k=k: to_sibling(parts[k], from_sib[k], k).start())
    to_sibling(c_part, c_sib, 8).start()
    to_sibling(m_part, m_sib, 9).start()

    def reduce_and_send(k):
        to_sibling(parts[k], from_sib[k], k).wait()
        staged[k][...] = (
            parts[k][me].astype(jnp.float32) + from_sib[k][...].astype(jnp.float32)
        ).astype(jnp.bfloat16)
        to_side(k).start()

    for k in order:
        at.when(k, lambda k=k: reduce_and_send(k))

    to_sibling(c_part, c_sib, 8).wait()
    acc[...] = c_part[me].astype(jnp.float32) + c_sib[...].astype(jnp.float32)
    to_sibling(m_part, m_sib, 9).wait()
    m_out[...] = (m_part[me].astype(jnp.float32) + m_sib[...].astype(jnp.float32)).astype(
        jnp.bfloat16
    )

    def arrive(k):
        dlat, dlon = SIDES[k]
        to_side(k).wait_send()
        pltpu.make_async_remote_copy(
            landed[k], landed[k], send.at[k], recv.at[k],
            device_id=at.sibling(), device_id_type=MESH,
        ).wait_recv()
        got = landed[k][...].astype(jnp.float32)
        if dlon:
            strip[(dlon + 1) // 2] += got
        elif dlat < 0:
            acc[0:RMAX] += got
        else:
            acc[rows - RMAX : rows] += got

    strip[...] = jnp.zeros_like(strip)
    for k in order:
        at.when(k, lambda k=k: arrive(k))
    for s, lo in ((0, 0), (1, cols - RMAX)):
        for n in range(rows):
            acc[n, lo : lo + RMAX, :] += strip[s, n * RMAX : (n + 1) * RMAX, :]
    g_out[...] = acc[...].astype(jnp.bfloat16)


def on_device(n_lat, n_lon, features, dilation_rates, branch_weight, branch_bias, merge_weight, cotangent):
    rows, cols, lanes = features.shape
    channels = merge_weight.shape[2]
    flat = strip_rows(rows)
    bf16, f32 = jnp.bfloat16, jnp.float32
    vmem = pl.BlockSpec(memory_space=pltpu.VMEM)
    hbm = pl.BlockSpec(memory_space=pl.ANY)

    def pack(strip):
        return jnp.pad(strip.reshape(rows * RMAX, lanes), ((0, flat - rows * RMAX), (0, 0)))

    def piece(k):
        return (RMAX, cols, lanes) if SIDES[k][1] == 0 else (flat, lanes)

    tile = jax.ShapeDtypeStruct((2, rows, cols, lanes), bf16)
    piece_pairs = [jax.ShapeDtypeStruct((2,) + piece(k), bf16) for k in range(8)]
    gathered = pl.pallas_call(
        functools.partial(gather_kernel, n_lat, n_lon, rows),
        out_shape=piece_pairs + [tile, tile],
        in_specs=[hbm] * 4,
        out_specs=[hbm] * 10,
        scratch_shapes=[
            pltpu.SemaphoreType.DMA((8,)),
            pltpu.SemaphoreType.DMA((8,)),
            pltpu.SemaphoreType.DMA((10,)),
            pltpu.SemaphoreType.DMA((10,)),
            pltpu.SemaphoreType.DMA((2,)),
        ],
        compiler_params=pltpu.CompilerParams(collective_id=0, has_side_effects=True),
        name="gather_halo",
    )(features, cotangent, pack(features[:, :RMAX]), pack(features[:, cols - RMAX :]))
    pieces, full_feat, full_cot = gathered[:8], gathered[8], gathered[9]

    lat = lax.axis_index("lat")
    info = jnp.concatenate(
        [
            dilation_rates,
            jnp.stack([lat > 0, lat < n_lat - 1]).astype(jnp.int32),
        ]
    )
    pad_cols = PADL + cols + 24
    padded_shape = (2, rows + 2 * RMAX, pad_cols, lanes)

    def whole(shape):
        return pl.BlockSpec(shape, lambda b, *_: (0,) * len(shape))

    outs = [tile, tile] + piece_pairs
    head = pl.pallas_call(
        functools.partial(head_kernel, rows, cols),
        out_shape=outs,
        grid_spec=pltpu.PrefetchScalarGridSpec(
            num_scalar_prefetch=1,
            grid=(BRANCHES,),
            in_specs=[
                pl.BlockSpec((1, 3, 3, channels, lanes), lambda b, *_: (b, 0, 0, 0, 0)),
                pl.BlockSpec((1, 1, lanes), lambda b, *_: (b, 0, 0)),
                pl.BlockSpec((1, lanes, channels), lambda b, *_: (b, 0, 0)),
                whole(tile.shape),
                whole(tile.shape),
            ]
            + [whole(s.shape) for s in piece_pairs],
            out_specs=[whole(s.shape) for s in outs],
            scratch_shapes=[
                pltpu.VMEM(padded_shape, f32),
                pltpu.VMEM(padded_shape, f32),
                pltpu.VMEM((rows * cols, channels), f32),
                pltpu.VMEM((flat, lanes), f32),
            ],
        ),
        compiler_params=pltpu.CompilerParams(vmem_limit_bytes=56 * 2**20),
        name="head",
    )(
        info,
        branch_weight,
        branch_bias.reshape(BRANCHES, 1, lanes),
        merge_weight,
        full_feat,
        full_cot,
        *pieces,
    )

    single = [pltpu.VMEM(piece(k), bf16) for k in range(8)]
    out = jax.ShapeDtypeStruct((rows, cols, lanes), bf16)
    return pl.pallas_call(
        functools.partial(scatter_kernel, n_lat, n_lon, rows, cols),
        out_shape=[out, out],
        in_specs=[vmem] * 10,
        out_specs=[vmem] * 2,
        scratch_shapes=single
        + single
        + single
        + [
            pltpu.VMEM((rows, cols, lanes), bf16),
            pltpu.VMEM((rows, cols, lanes), bf16),
            pltpu.VMEM((rows, cols, lanes), f32),
            pltpu.VMEM((2, flat, lanes), f32),
            pltpu.SemaphoreType.DMA((8,)),
            pltpu.SemaphoreType.DMA((8,)),
            pltpu.SemaphoreType.DMA((10,)),
            pltpu.SemaphoreType.DMA((10,)),
        ],
        compiler_params=pltpu.CompilerParams(
            collective_id=1, has_side_effects=True, vmem_limit_bytes=40 * 2**20
        ),
        name="scatter_halo",
    )(*head)


def solution(mesh):
    spec = P(("grp", "lat"), "lon", "ch")
    return jax.shard_map(
        functools.partial(on_device, mesh.shape["lat"], mesh.shape["lon"]),
        mesh=mesh,
        in_specs=(
            spec,
            P(),
            P(None, None, None, None, "ch"),
            P(None, "ch"),
            P(None, "ch", None),
            spec,
        ),
        out_specs=(spec, spec),
        check_vma=False,
    )
```

time: 276 us -> 117 us (0.42); the launches traced: 272 us -> 117 us
  Pallas kernels: 0 us -> 99.4 us
  waiting for transfers between devices: 94.5 us -> 0 us
  local copies, waits for them, and re-layouts: 64.9 us -> 15.4 us
  matrix products: 37.5 us -> 0 us
  between operations: 36.9 us -> 0.68 us
  starting transfers between devices: 19.2 us -> 0 us
  other arithmetic: 13.8 us -> 1.31 us
  blocking collectives: 5.16 us -> 0 us
    pallas_call x0 -> x3, Pallas kernels: none -> 99.4 us  [the longest x1 49.7 us: on_device(): pl.pallas_call(functools.partial(head_kernel, rows, cols), out_shape=outs...]
    ppermute x8 -> x0, waiting for transfers between devices: 89.9 us -> none  [the longest x4 62.8 us: with_halo(): lax.ppermute(tail, axis, [(i, (i + 1) % count) for i in range(ends)])]
    dot_general x20 -> x0, matrix products: 37.5 us -> none  [the longest x5 16.4 us: on_device(): jnp.dot(patches, branch_weight[b].reshape(9 * channels, own_out), preferr...]
    unnamed x60 -> x22, local copies, waits for them, and re-layouts: 36.3 us -> 11.6 us
    ppermute x8 -> x0, starting transfers between devices: 19.1 us -> none  [the longest x4 12.3 us: with_halo(): lax.ppermute(tail, axis, [(i, (i + 1) % count) for i in range(ends)])]
    transpose x6 -> x0, local copies, waits for them, and re-layouts: 15.2 us -> none  [on_device(): jnp.transpose(branch_weight[b], (0, 1, 3, 2)).reshape(9 * own_out, channels)]
    concatenate x4 -> x1, other arithmetic: 9.9 us -> 1.23 us  [on_device(): jnp.concatenate([dilation_rates, jnp.stack([lat > 0, lat < n_lat - 1]).as...]
    concatenate x3 -> x0, local copies, waits for them, and re-layouts: 7.57 us -> none  [the longest x1 3.55 us: on_device(): patches = jnp.concatenate(pieces, axis=2).reshape(cells, 9 * channels)]
  transfers between devices with their start and end apart: 10 -> 0, of which waited for: 9 -> 0; matrix products, arithmetic and copies ran while one was open for 17% -> 0% of each run, Pallas kernels for 0% -> 0%
where the time goes in v1:
time: 117 us
  Pallas kernels  99.4 us (85%)
  local copies, waits for them, and re-layouts  15.4 us (13%)
  other arithmetic  1.31 us (1%)
    pallas_call x1, Pallas kernels, on_device(): pl.pallas_call(functools.partial(head_kernel, rows, cols), out_shape=outs...  49.7 us
    pallas_call x1, Pallas kernels, on_device(): pl.pallas_call(functools.partial(gather_kernel, n_lat, n_lon, rows), out_...  31.2 us
    pallas_call x1, Pallas kernels, on_device(): pl.pallas_call(functools.partial(scatter_kernel, n_lat, n_lon, rows, cols...  18.5 us
    unnamed x22, local copies, waits for them, and re-layouts  11.6 us

profile of v1, /device:TPU:0, one launch (start us, length us, event | category | flops | bytes accessed | tf_op | source)
XLA Modules:
  0.0 116.8 jit_solution(410299387040364529)
XLA Ops:
  0.6 0.1 add_convert_fusion
  0.7 1.2 %pad_add_fusion.info = s32[7]{0:T(128)} fusion(s32[2]{0:T(128)S(1)} %add_convert_fusion, s32[5]{0:T(128)} %param.7), kind=kLoop, calls=%fused_computation.1 | loop fusion | flops 7 | bytes 56 | tf_op jit(solution)/shard_map/concatenate | solution.py:400
  1.9 1.3 %reshape.13.bias = f32[5,1,128]{2,1,0:T(1,128)} reshape(f32[5,128]{1,0:T(8,128)} %param.9) | data formatting | bytes 5120 | tf_op jit(solution)/shard_map/reshape | solution.py:440
  3.2 1.0 fusion
  4.3 0.1 reshape.15
  4.3 0.7 pad.8.right
  5.0 0.1 reshape.14
  5.1 0.7 pad.7.left
  5.7 31.2 %gather_halo.1 = (bf16[2,21,64,128]{3,2,1,0:T(8,128)(2,1)}, bf16[2,21,64,128]{3,2,1,0:T(8,128)(2,1)}, bf16[2,512,128]{2,1,0:T(8,128)(2,1)}, bf16[2,512,128]{2,1,...) custom-call(bf16[24,64,128]{2,1,0:T(8,128)(2,1)} %feat.1, ...), custom_call_target="tpu_custom_call" | custom-call | tf_op jit(solution)/shard_map/gather_halo/pallas_call | solution.py:382
  37.0 49.7 %head.1 = (bf16[2,24,64,128]{3,2,1,0:T(8,128)(2,1)}, bf16[2,24,64,128]{3,2,1,0:T(8,128)(2,1)}, bf16[2,21,64,128]{3,2,1,0:T(8,128)(2,1)}, bf16[2,21,64,128]{3,2,1...) custom-call(s32[7]{0:T(128)} %pad_add_fusion.info, ...), custom_call_target="tpu_custom_call" | custom-call | tf_op jit(solution)/shard_map/head/pallas_call | solution.py:413
  86.7 0.0 copy-start
  86.7 1.1 copy-done
  87.8 1.1 copy-done.1
  88.9 1.1 copy-done.2
  90.0 1.1 copy-done.3
  91.1 0.9 copy-done.4
  92.1 0.9 copy-done.5
  93.0 0.9 copy-done.6
  94.0 0.9 copy-done.7
  94.9 0.9 copy-done.8
  95.9 0.9 copy-done.9
  96.8 18.5 %scatter_halo.1 = (bf16[24,64,128]{2,1,0:T(8,128)(2,1)S(1)}, bf16[24,64,128]{2,1,0:T(8,128)(2,1)S(1)}) custom-call(bf16[2,24,64,128]{3,2,1,0:T(8,128)(2,1)S(1)} %copy-done, bf16[2,24,64,128]{3,2,1,0:T(8,128)(2,1)S(1)} %copy-done.1, bf16[2,21,64,128]{3,2,1,0:T(8,128)(2,1)S(1)} %copy-done.2, bf16[2,21,64,128]{3,2,1,0:T(8,128)(2,1)S(1)} %copy-done.3, ...), custom_call_target="tpu_custom_call" | custom-call | tf_op jit(solution)/shard_map/scatter_halo/pallas_call | solution.py:449
  115.3 0.7 copy.10
  116.1 0.7 copy.11
  (9 shorter events, 0.0 us)
Async XLA Ops:
  86.7 1.1 copy-start
  87.8 1.1 copy-start.1
  88.9 1.1 copy-start.2
  90.0 1.1 copy-start.3
  91.1 0.9 copy-start.4
  92.1 0.9 copy-start.5
  93.0 0.9 copy-start.6
  94.0 0.9 copy-start.7
  94.9 0.9 copy-start.8
  95.9 0.9 copy-start.9

commit v2 on v1

--- a/solution.py
+++ b/solution.py
@@ -23,6 +23,9 @@
 
 def strip_rows(rows):
     return (rows * RMAX + 15) // 16 * 16
+
+
+CORNER = strip_rows(RMAX)
 
 
 class Where:
@@ -65,21 +68,26 @@
         )
 
 
-def gather_kernel(n_lat, n_lon, rows, feat, cot, left, right, *refs):
+def gather_kernel(n_lat, n_lon, rows, cols, feat, cot, *refs):
     pieces = refs[:8]
     full_feat, full_cot = refs[8:10]
-    send, recv, send2, recv2, local = refs[10:]
+    packed = refs[10:16]
+    wide, strip, send, recv, send2, recv2, local = refs[16:]
     at = Where(n_lat, n_lon)
     me = at.ch
+    copies = []
+    for n, (src, dst) in enumerate(((feat, full_feat), (cot, full_cot))):
+        copies.append(pltpu.make_async_copy(src, dst.at[me], local.at[n]))
+        copies[-1].start()
     at.barrier()
+    copies[0].wait()
 
     def source(k):
         dlat, dlon = SIDES[k]
-        if dlon < 0:
-            return left
-        if dlon > 0:
-            return right
-        return feat.at[pl.ds(0, RMAX)] if dlat < 0 else feat.at[pl.ds(rows - RMAX, RMAX)]
+        if dlon:
+            return packed[k - 2]
+        own = full_feat.at[me]
+        return own.at[pl.ds(0, RMAX)] if dlat < 0 else own.at[pl.ds(rows - RMAX, RMAX)]
 
     def to_side(k):
         return pltpu.make_async_remote_copy(
@@ -101,15 +109,26 @@
             device_id_type=MESH,
         )
 
-    order = (4, 5, 6, 7, 0, 1, 2, 3)
-    for k in order:
+    for k in (0, 1):
         at.when(k, lambda k=k: to_side(k).start())
+    wide[...] = full_feat[me].astype(jnp.float32)
+    far = (rows - RMAX) * RMAX
+    strip[...] = jnp.zeros_like(strip)
+    for s, lo in ((0, 0), (1, cols - RMAX)):
+        for n in range(rows):
+            strip[s, n * RMAX : (n + 1) * RMAX, :] = wide[n, lo : lo + RMAX, :]
+        for k in (2 + s, 4 + s, 6 + s):
+            start, size = {2: (0, strip.shape[1]), 4: (0, CORNER), 6: (far, CORNER)}[k - s]
+            packed[k - 2][...] = strip[s, start : start + size, :].astype(jnp.bfloat16)
+            at.when(k, lambda k=k: to_side(k).start())
     own = []
-    for n, (src, dst) in enumerate(((feat, full_feat), (cot, full_cot))):
+    for n, full in enumerate((full_feat, full_cot)):
+        if n:
+            copies[n].wait()
         own.append(
             pltpu.make_async_remote_copy(
-                src,
-                dst.at[me],
+                full.at[me],
+                full.at[me],
                 send2.at[8 + n],
                 recv2.at[8 + n],
                 device_id=at.sibling(),
@@ -117,10 +136,6 @@
             )
         )
         own[-1].start()
-    copies = []
-    for n, (src, dst) in enumerate(((feat, full_feat), (cot, full_cot))):
-        copies.append(pltpu.make_async_copy(src, dst.at[me], local.at[n]))
-        copies[-1].start()
 
     def arrive(k):
         pltpu.make_async_remote_copy(
@@ -160,20 +175,19 @@
             device_id=at.sibling(),
             device_id_type=MESH,
         ).wait_recv()
-        copies[n].wait()
 
 
 def head_kernel(
-    rows, cols, info, weight, bias, merge, feat, cot, p0, p1, p2, p3, p4, p5, p6, p7,
+    rows, cols, n_lat, info, weight, bias, merge, feat, cot, p0, p1, p2, p3, p4, p5, p6, p7,
     m_out, c_out, g0, g1, g2, g3, g4, g5, g6, g7, padded, total, merged, strip,
 ):
     b = pl.program_id(0)
     pieces = (p0, p1, p2, p3, p4, p5, p6, p7)
     grads = (g0, g1, g2, g3, g4, g5, g6, g7)
     all_rows = rows + 2 * RMAX
-    has_up, has_down = info[BRANCHES] > 0, info[BRANCHES + 1] > 0
+    lat = lax.axis_index("lat")
+    has_up, has_down = lat > 0, lat < n_lat - 1
     right_col = PADL + cols
-    near = rows * RMAX
 
     @pl.when(b == 0)
     def _():
@@ -183,7 +197,6 @@
                 dlat, dlon = SIDES[k]
                 top = {-1: 0, 0: RMAX, 1: RMAX + rows}[dlat]
                 count = rows if dlat == 0 else RMAX
-                skip = rows - RMAX if dlat < 0 else 0
                 if dlon == 0:
                     lo, hi = PADL, right_col
                 elif dlon < 0:
@@ -191,13 +204,14 @@
                 else:
                     lo, hi = right_col, right_col + RMAX
 
-                def fill(k=k, c=c, top=top, count=count, skip=skip, lo=lo, hi=hi, dlon=dlon):
+                def fill(k=k, c=c, top=top, count=count, lo=lo, hi=hi, dlat=dlat, dlon=dlon):
                     if dlon == 0:
                         padded[c, top : top + count, lo:hi, :] = pieces[k][c].astype(jnp.float32)
                     else:
-                        strip[...] = pieces[k][c].astype(jnp.float32)
+                        size = CORNER if dlat else strip.shape[0]
+                        strip[0:size, :] = pieces[k][c].astype(jnp.float32)
                         for n in range(count):
-                            start = (skip + n) * RMAX
+                            start = n * RMAX
                             padded[c, top + n, lo:hi, :] = strip[start : start + RMAX, :]
 
                 if dlat == 0:
@@ -235,7 +249,7 @@
             weight[0].reshape(9 * 2 * LANES, LANES),
             preferred_element_type=jnp.float32,
         )
-        preact = preact + bias[0]
+        preact = preact + bias[pl.ds(b, 1), :]
         sigma = 1.0 / (1.0 + jnp.exp(-preact))
         activated = (preact * sigma).astype(jnp.bfloat16)
         here = pl.ds(pl.multiple_of(row * cols, cells), cells)
@@ -279,7 +293,6 @@
                 dlat, dlon = SIDES[k]
                 top = {-1: 0, 0: RMAX, 1: RMAX + rows}[dlat]
                 count = rows if dlat == 0 else RMAX
-                skip = rows - RMAX if dlat < 0 else 0
                 if dlon == 0:
                     grads[k][c] = total[c, top : top + count, PADL:right_col, :].astype(
                         jnp.bfloat16
@@ -288,9 +301,10 @@
                 lo = PADL - RMAX if dlon < 0 else right_col
                 strip[...] = jnp.zeros_like(strip)
                 for n in range(count):
-                    start = (skip + n) * RMAX
+                    start = n * RMAX
                     strip[start : start + RMAX, :] = total[c, top + n, lo : lo + RMAX, :]
-                grads[k][c] = strip[...].astype(jnp.bfloat16)
+                size = CORNER if dlat else strip.shape[0]
+                grads[k][c] = strip[0:size, :].astype(jnp.bfloat16)
 
 
 def scatter_kernel(n_lat, n_lon, rows, cols, m_part, c_part, *refs):
@@ -348,7 +362,8 @@
         ).wait_recv()
         got = landed[k][...].astype(jnp.float32)
         if dlon:
-            strip[(dlon + 1) // 2] += got
+            start = (rows - RMAX) * RMAX if dlat > 0 else 0
+            strip[(dlon + 1) // 2, start : start + got.shape[0], :] += got
         elif dlat < 0:
             acc[0:RMAX] += got
         else:
@@ -371,60 +386,53 @@
     vmem = pl.BlockSpec(memory_space=pltpu.VMEM)
     hbm = pl.BlockSpec(memory_space=pl.ANY)
 
-    def pack(strip):
-        return jnp.pad(strip.reshape(rows * RMAX, lanes), ((0, flat - rows * RMAX), (0, 0)))
-
     def piece(k):
-        return (RMAX, cols, lanes) if SIDES[k][1] == 0 else (flat, lanes)
+        dlat, dlon = SIDES[k]
+        if dlon == 0:
+            return (RMAX, cols, lanes)
+        return (CORNER if dlat else flat, lanes)
 
     tile = jax.ShapeDtypeStruct((2, rows, cols, lanes), bf16)
     piece_pairs = [jax.ShapeDtypeStruct((2,) + piece(k), bf16) for k in range(8)]
     gathered = pl.pallas_call(
-        functools.partial(gather_kernel, n_lat, n_lon, rows),
+        functools.partial(gather_kernel, n_lat, n_lon, rows, cols),
         out_shape=piece_pairs + [tile, tile],
-        in_specs=[hbm] * 4,
-        out_specs=[hbm] * 10,
-        scratch_shapes=[
+        in_specs=[hbm] * 2,
+        out_specs=[vmem] * 10,
+        scratch_shapes=[pltpu.VMEM(piece(k), bf16) for k in range(2, 8)]
+        + [
+            pltpu.VMEM((rows, cols, lanes), f32),
+            pltpu.VMEM((2, flat, lanes), f32),
             pltpu.SemaphoreType.DMA((8,)),
             pltpu.SemaphoreType.DMA((8,)),
             pltpu.SemaphoreType.DMA((10,)),
             pltpu.SemaphoreType.DMA((10,)),
             pltpu.SemaphoreType.DMA((2,)),
         ],
-        compiler_params=pltpu.CompilerParams(collective_id=0, has_side_effects=True),
+        compiler_params=pltpu.CompilerParams(
+            collective_id=0, has_side_effects=True, vmem_limit_bytes=24 * 2**20
+        ),
         name="gather_halo",
-    )(features, cotangent, pack(features[:, :RMAX]), pack(features[:, cols - RMAX :]))
+    )(features, cotangent)
     pieces, full_feat, full_cot = gathered[:8], gathered[8], gathered[9]
 
-    lat = lax.axis_index("lat")
-    info = jnp.concatenate(
-        [
-            dilation_rates,
-            jnp.stack([lat > 0, lat < n_lat - 1]).astype(jnp.int32),
-        ]
-    )
     pad_cols = PADL + cols + 24
     padded_shape = (2, rows + 2 * RMAX, pad_cols, lanes)
 
-    def whole(shape):
-        return pl.BlockSpec(shape, lambda b, *_: (0,) * len(shape))
-
     outs = [tile, tile] + piece_pairs
     head = pl.pallas_call(
-        functools.partial(head_kernel, rows, cols),
+        functools.partial(head_kernel, rows, cols, n_lat),
         out_shape=outs,
         grid_spec=pltpu.PrefetchScalarGridSpec(
             num_scalar_prefetch=1,
             grid=(BRANCHES,),
             in_specs=[
                 pl.BlockSpec((1, 3, 3, channels, lanes), lambda b, *_: (b, 0, 0, 0, 0)),
-                pl.BlockSpec((1, 1, lanes), lambda b, *_: (b, 0, 0)),
+                vmem,
                 pl.BlockSpec((1, lanes, channels), lambda b, *_: (b, 0, 0)),
-                whole(tile.shape),
-                whole(tile.shape),
             ]
-            + [whole(s.shape) for s in piece_pairs],
-            out_specs=[whole(s.shape) for s in outs],
+            + [vmem] * 10,
+            out_specs=[vmem] * 10,
             scratch_shapes=[
                 pltpu.VMEM(padded_shape, f32),
                 pltpu.VMEM(padded_shape, f32),
@@ -432,12 +440,12 @@
                 pltpu.VMEM((flat, lanes), f32),
             ],
         ),
-        compiler_params=pltpu.CompilerParams(vmem_limit_bytes=56 * 2**20),
+        compiler_params=pltpu.CompilerParams(vmem_limit_bytes=32 * 2**20),
         name="head",
     )(
-        info,
+        dilation_rates,
         branch_weight,
-        branch_bias.reshape(BRANCHES, 1, lanes),
+        branch_bias,
         merge_weight,
         full_feat,
         full_cot,
@@ -465,7 +473,7 @@
             pltpu.SemaphoreType.DMA((10,)),
         ],
         compiler_params=pltpu.CompilerParams(
-            collective_id=1, has_side_effects=True, vmem_limit_bytes=40 * 2**20
+            collective_id=1, has_side_effects=True, vmem_limit_bytes=24 * 2**20
         ),
         name="scatter_halo",
     )(*head)

time: 117 us -> 93.1 us (0.80)
  Pallas kernels: 99.4 us -> 84.5 us
  local copies, waits for them, and re-layouts: 15.4 us -> 7.62 us
  other arithmetic: 1.31 us -> 0 us
    pallas_call x2, Pallas kernels: 80.9 us -> 66.4 us  [the longest x1 44.8 us: on_device(): pl.pallas_call(functools.partial(head_kernel, rows, cols, n_lat), out_sha...]
    unnamed x22 -> x14, local copies, waits for them, and re-layouts: 11.6 us -> 7.62 us
    reshape x3 -> x0, local copies, waits for them, and re-layouts: 1.39 us -> none  [the longest x1 1.28 us: on_device(): branch_bias.reshape(BRANCHES, 1, lanes)]
    pad x2 -> x0, local copies, waits for them, and re-layouts: 1.33 us -> none  [pack(): jnp.pad(strip.reshape(rows * RMAX, lanes), ((0, flat - rows * RMAX), (0,...]
    concatenate x1 -> x0, other arithmetic: 1.23 us -> none  [on_device(): jnp.concatenate([dilation_rates, jnp.stack([lat > 0, lat < n_lat - 1]).as...]
where the time goes in v2:
time: 93.1 us; the launch traced here: 92.8 us
  Pallas kernels  84.5 us (91%)
  local copies, waits for them, and re-layouts  7.62 us (8%)
    pallas_call x1, Pallas kernels, on_device(): pl.pallas_call(functools.partial(head_kernel, rows, cols, n_lat), out_sha...  44.8 us
    pallas_call x1, Pallas kernels, on_device(): pl.pallas_call(functools.partial(gather_kernel, n_lat, n_lon, rows, cols)...  21.6 us
    pallas_call x1, Pallas kernels, on_device(): pl.pallas_call(functools.partial(scatter_kernel, n_lat, n_lon, rows, cols...  18.1 us
    unnamed x14, local copies, waits for them, and re-layouts  7.62 us

profile of v2, /device:TPU:0, one launch (start us, length us, event | category | flops | bytes accessed | tf_op | source)
XLA Modules:
  0.0 92.8 jit_solution(11146420552581706197)
XLA Ops:
  0.6 0.0 copy-start.1
  0.6 1.0 %copy-done.1 = bf16[24,64,128]{2,1,0:T(8,128)(2,1)S(1)} copy-done((bf16[24,64,128]{2,1,0:T(8,128)(2,1)S(1)}, bf16[24,64,128]{2,1,0:T(8,128)(2,1)}, u32[]{:S(2)}) %copy-start.1) | copy-done | bytes 393240
  1.6 0.0 copy-start.2
  1.6 1.0 %copy-done.2 = bf16[24,64,128]{2,1,0:T(8,128)(2,1)S(1)} copy-done((bf16[24,64,128]{2,1,0:T(8,128)(2,1)S(1)}, bf16[24,64,128]{2,1,0:T(8,128)(2,1)}, u32[]{:S(2)}) %copy-start.2) | copy-done | bytes 393240
  2.6 21.6 %gather_halo.1 = (bf16[2,21,64,128]{3,2,1,0:T(8,128)(2,1)S(1)}, bf16[2,21,64,128]{3,2,1,0:T(8,128)(2,1)S(1)}, bf16[2,512,128]{2,1,0:T(8,128)(2,1)S(1)}, bf16[2,5...) custom-call(bf16[24,64,128]{2,1,0:T(8,128)(2,1)S(1)} %copy-done.1, ...), custom_call_target="tpu_custom_call" | custom-call | tf_op jit(solution)/shard_map/gather_halo/pallas_call | solution.py:397
  24.2 0.0 copy-start
  24.2 1.8 %copy-done = bf16[5,3,3,256,128]{4,3,2,1,0:T(8,128)(2,1)S(1)} copy-done((bf16[5,3,3,256,128]{4,3,2,1,0:T(8,128)(2,1)S(1)}, bf16[5,3,3,256,128]{4,3,2,1,0:T(8,128)(2,1)}, u32[]{:S(2)}) %copy-start) | copy-done | bytes 2949144
  26.1 0.0 copy-start.3
  26.1 1.0 %copy-done.3 = bf16[5,128,256]{2,1,0:T(8,128)(2,1)S(1)} copy-done((bf16[5,128,256]{2,1,0:T(8,128)(2,1)S(1)}, bf16[5,128,256]{2,1,0:T(8,128)(2,1)}, u32[]{:S(2)}) %copy-start.3) | copy-done | bytes 327704
  27.0 0.0 copy-start.4
  27.0 0.7 copy-done.4
  27.7 0.0 copy-start.5
  27.7 0.7 copy-done.5
  28.4 44.8 %head.1 = (bf16[2,24,64,128]{3,2,1,0:T(8,128)(2,1)S(1)}, bf16[2,24,64,128]{3,2,1,0:T(8,128)(2,1)S(1)}, bf16[2,21,64,128]{3,2,1,0:T(8,128)(2,1)S(1)}, bf16[2,21,6...) custom-call(s32[5]{0:T(128)S(1)} %copy-done.5, ...), custom_call_target="tpu_custom_call" | custom-call | tf_op jit(solution)/shard_map/head/pallas_call | solution.py:423
  73.2 18.1 %scatter_halo.1 = (bf16[24,64,128]{2,1,0:T(8,128)(2,1)S(1)}, bf16[24,64,128]{2,1,0:T(8,128)(2,1)S(1)}) custom-call(bf16[2,24,64,128]{3,2,1,0:T(8,128)(2,1)S(1)} %get-tuple-element.32.m_part, bf16[2,24,64,128]{3,2,1,0:T(8,128)(2,1)S(1)} %get-tuple-element.33.c_part, bf16[2,21,64,128]{3,2,1,0:T(8,128)(2,1)S(1)} %get-tuple-element.34.refs_0_, ...), custom_call_target="tpu_custom_call" | custom-call | tf_op jit(solution)/shard_map/scatter_halo/pallas_call | solution.py:457
  91.3 0.7 copy.10
  92.1 0.7 copy.11
Async XLA Ops:
  0.6 1.0 %copy-start.1 = (bf16[24,64,128]{2,1,0:T(8,128)(2,1)S(1)}, bf16[24,64,128]{2,1,0:T(8,128)(2,1)}, u32[]{:S(2)}) copy-start(bf16[24,64,128]{2,1,0:T(8,128)(2,1)} %feat.1) | copy-start | bytes 1179652
  1.6 1.0 %copy-start.2 = (bf16[24,64,128]{2,1,0:T(8,128)(2,1)S(1)}, bf16[24,64,128]{2,1,0:T(8,128)(2,1)}, u32[]{:S(2)}) copy-start(bf16[24,64,128]{2,1,0:T(8,128)(2,1)} %cot.1) | copy-start | bytes 1179652
  24.2 1.8 %copy-start = (bf16[5,3,3,256,128]{4,3,2,1,0:T(8,128)(2,1)S(1)}, bf16[5,3,3,256,128]{4,3,2,1,0:T(8,128)(2,1)}, u32[]{:S(2)}) copy-start(bf16[5,3,3,256,128]{4,3,2,1,0:T(8,128)(2,1)} %weight.1) | copy-start | bytes 8847364
  26.1 1.0 %copy-start.3 = (bf16[5,128,256]{2,1,0:T(8,128)(2,1)S(1)}, bf16[5,128,256]{2,1,0:T(8,128)(2,1)}, u32[]{:S(2)}) copy-start(bf16[5,128,256]{2,1,0:T(8,128)(2,1)} %merge.1) | copy-start | bytes 983044
  27.0 0.7 copy-start.4
  27.7 0.7 copy-start.5

commit v3 on v2

--- a/solution.py
+++ b/solution.py
@@ -12,7 +12,6 @@
 PADL = 24
 LANES = 128
 MESH = pl.DeviceIdType.MESH
-ROW_CHUNK = 8
 
 SIDES = ((-1, 0), (1, 0), (0, -1), (0, 1), (-1, -1), (-1, 1), (1, -1), (1, 1))
 
@@ -68,15 +67,17 @@
         )
 
 
-def gather_kernel(n_lat, n_lon, rows, cols, feat, cot, *refs):
+def gather_kernel(n_lat, n_lon, rows, cols, *refs):
+    owns, refs = refs[:5], refs[5:]
     pieces = refs[:8]
-    full_feat, full_cot = refs[8:10]
-    packed = refs[10:16]
-    wide, strip, send, recv, send2, recv2, local = refs[16:]
+    fulls = refs[8:13]
+    full_feat = fulls[0]
+    packed = refs[13:19]
+    wide, strip, send, recv, send2, recv2, local = refs[19:]
     at = Where(n_lat, n_lon)
     me = at.ch
     copies = []
-    for n, (src, dst) in enumerate(((feat, full_feat), (cot, full_cot))):
+    for n, (src, dst) in enumerate(zip(owns, fulls)):
         copies.append(pltpu.make_async_copy(src, dst.at[me], local.at[n]))
         copies[-1].start()
     at.barrier()
@@ -122,7 +123,7 @@
             packed[k - 2][...] = strip[s, start : start + size, :].astype(jnp.bfloat16)
             at.when(k, lambda k=k: to_side(k).start())
     own = []
-    for n, full in enumerate((full_feat, full_cot)):
+    for n, full in enumerate(fulls):
         if n:
             copies[n].wait()
         own.append(
@@ -165,7 +166,7 @@
 
     for k in range(8):
         at.when(k, lambda k=k: other_arrives(k))
-    for n, dst in enumerate((full_feat, full_cot)):
+    for n, dst in enumerate(fulls):
         own[n].wait_send()
         pltpu.make_async_remote_copy(
             dst.at[1 - me],
@@ -186,6 +187,7 @@
     grads = (g0, g1, g2, g3, g4, g5, g6, g7)
     all_rows = rows + 2 * RMAX
     lat = lax.axis_index("lat")
+    first_row = lax.axis_index("ch") * (rows // 2)
     has_up, has_down = lat > 0, lat < n_lat - 1
     right_col = PADL + cols
 
@@ -229,56 +231,52 @@
         merged[...] = jnp.zeros_like(merged)
 
     rate = info[b]
-    cells = ROW_CHUNK * cols
-
-    def chunk(n, _):
-        row = n * ROW_CHUNK
-        taps = []
-        for i in range(3):
-            for j in range(3):
-                for c in range(2):
-                    tap = padded[
-                        c,
-                        pl.ds(row + RMAX + rate * (i - 1), ROW_CHUNK),
-                        pl.ds(PADL + rate * (j - 1), cols),
-                        :,
-                    ]
-                    taps.append(tap.reshape(cells, LANES).astype(jnp.bfloat16))
-        preact = jnp.dot(
-            jnp.concatenate(taps, axis=1),
-            weight[0].reshape(9 * 2 * LANES, LANES),
-            preferred_element_type=jnp.float32,
-        )
-        preact = preact + bias[pl.ds(b, 1), :]
-        sigma = 1.0 / (1.0 + jnp.exp(-preact))
-        activated = (preact * sigma).astype(jnp.bfloat16)
-        here = pl.ds(pl.multiple_of(row * cols, cells), cells)
-        merged[here, :] += jnp.dot(activated, merge[0], preferred_element_type=jnp.float32)
-        own_cot = jnp.concatenate(
-            [cot[c, pl.ds(row, ROW_CHUNK)].reshape(cells, LANES) for c in range(2)], axis=1
-        )
-        dact = lax.dot_general(
-            own_cot, merge[0], (((1,), (1,)), ((), ())), preferred_element_type=jnp.float32
-        )
-        dpre = (dact * (sigma * (1.0 + preact * (1.0 - sigma)))).astype(jnp.bfloat16)
-        for i in range(3):
-            for j in range(3):
-                part = lax.dot_general(
-                    dpre,
-                    weight[0, i, j],
-                    (((1,), (1,)), ((), ())),
-                    preferred_element_type=jnp.float32,
-                )
-                for c in range(2):
-                    total[
-                        c,
-                        pl.ds(row + RMAX + rate * (i - 1), ROW_CHUNK),
-                        pl.ds(PADL + rate * (j - 1), cols),
-                        :,
-                    ] += part[:, c * LANES : (c + 1) * LANES].reshape(ROW_CHUNK, cols, LANES)
-        return 0
-
-    lax.fori_loop(0, rows // ROW_CHUNK, chunk, 0)
+    own_rows = rows // 2
+    cells = own_rows * cols
+    taps = []
+    for i in range(3):
+        for j in range(3):
+            for c in range(2):
+                tap = padded[
+                    c,
+                    pl.ds(first_row + RMAX + rate * (i - 1), own_rows),
+                    pl.ds(PADL + rate * (j - 1), cols),
+                    :,
+                ]
+                taps.append(tap.reshape(cells, LANES).astype(jnp.bfloat16))
+    kernel = jnp.concatenate(
+        [weight[h, b].reshape(9 * 2 * LANES, LANES) for h in range(2)], axis=1
+    )
+    preact = jnp.dot(
+        jnp.concatenate(taps, axis=1), kernel, preferred_element_type=jnp.float32
+    )
+    preact = preact + jnp.concatenate([bias[h, pl.ds(b, 1), :] for h in range(2)], axis=1)
+    sigma = 1.0 / (1.0 + jnp.exp(-preact))
+    activated = (preact * sigma).astype(jnp.bfloat16)
+    project = jnp.concatenate([merge[h, b] for h in range(2)], axis=0)
+    here = pl.ds(pl.multiple_of(first_row * cols, cells), cells)
+    merged[here, :] += jnp.dot(activated, project, preferred_element_type=jnp.float32)
+    own_cot = jnp.concatenate(
+        [cot[c, pl.ds(first_row, own_rows)].reshape(cells, LANES) for c in range(2)], axis=1
+    )
+    transposed = (((1,), (1,)), ((), ()))
+    dact = lax.dot_general(own_cot, project, transposed, preferred_element_type=jnp.float32)
+    dpre = (dact * (sigma * (1.0 + preact * (1.0 - sigma)))).astype(jnp.bfloat16)
+    for i in range(3):
+        for j in range(3):
+            part = lax.dot_general(
+                dpre,
+                jnp.concatenate([weight[h, b, i, j] for h in range(2)], axis=1),
+                transposed,
+                preferred_element_type=jnp.float32,
+            )
+            for c in range(2):
+                total[
+                    c,
+                    pl.ds(first_row + RMAX + rate * (i - 1), own_rows),
+                    pl.ds(PADL + rate * (j - 1), cols),
+                    :,
+                ] += part[:, c * LANES : (c + 1) * LANES].reshape(own_rows, cols, LANES)
 
     @pl.when(b == BRANCHES - 1)
     def _():
@@ -384,7 +382,7 @@
     flat = strip_rows(rows)
     bf16, f32 = jnp.bfloat16, jnp.float32
     vmem = pl.BlockSpec(memory_space=pltpu.VMEM)
-    hbm = pl.BlockSpec(memory_space=pl.ANY)
+    hbm = pl.BlockSpec(memory_space=pltpu.HBM)
 
     def piece(k):
         dlat, dlon = SIDES[k]
@@ -394,27 +392,29 @@
 
     tile = jax.ShapeDtypeStruct((2, rows, cols, lanes), bf16)
     piece_pairs = [jax.ShapeDtypeStruct((2,) + piece(k), bf16) for k in range(8)]
+    own = (features, cotangent, branch_weight, merge_weight, branch_bias)
     gathered = pl.pallas_call(
         functools.partial(gather_kernel, n_lat, n_lon, rows, cols),
-        out_shape=piece_pairs + [tile, tile],
-        in_specs=[hbm] * 2,
-        out_specs=[vmem] * 10,
+        out_shape=piece_pairs + [jax.ShapeDtypeStruct((2,) + a.shape, a.dtype) for a in own],
+        in_specs=[hbm] * 5,
+        out_specs=[vmem] * 13,
         scratch_shapes=[pltpu.VMEM(piece(k), bf16) for k in range(2, 8)]
         + [
             pltpu.VMEM((rows, cols, lanes), f32),
             pltpu.VMEM((2, flat, lanes), f32),
             pltpu.SemaphoreType.DMA((8,)),
             pltpu.SemaphoreType.DMA((8,)),
-            pltpu.SemaphoreType.DMA((10,)),
-            pltpu.SemaphoreType.DMA((10,)),
-            pltpu.SemaphoreType.DMA((2,)),
+            pltpu.SemaphoreType.DMA((13,)),
+            pltpu.SemaphoreType.DMA((13,)),
+            pltpu.SemaphoreType.DMA((5,)),
         ],
         compiler_params=pltpu.CompilerParams(
             collective_id=0, has_side_effects=True, vmem_limit_bytes=24 * 2**20
         ),
         name="gather_halo",
-    )(features, cotangent)
+    )(*own)
     pieces, full_feat, full_cot = gathered[:8], gathered[8], gathered[9]
+    weights, merges, biases = gathered[10:]
 
     pad_cols = PADL + cols + 24
     padded_shape = (2, rows + 2 * RMAX, pad_cols, lanes)
@@ -426,12 +426,7 @@
         grid_spec=pltpu.PrefetchScalarGridSpec(
             num_scalar_prefetch=1,
             grid=(BRANCHES,),
-            in_specs=[
-                pl.BlockSpec((1, 3, 3, channels, lanes), lambda b, *_: (b, 0, 0, 0, 0)),
-                vmem,
-                pl.BlockSpec((1, lanes, channels), lambda b, *_: (b, 0, 0)),
-            ]
-            + [vmem] * 10,
+            in_specs=[vmem] * 13,
             out_specs=[vmem] * 10,
             scratch_shapes=[
                 pltpu.VMEM(padded_shape, f32),
@@ -444,9 +439,9 @@
         name="head",
     )(
         dilation_rates,
-        branch_weight,
-        branch_bias,
-        merge_weight,
+        weights,
+        biases,
+        merges,
         full_feat,
         full_cot,
         *pieces,

time: 93.1 us -> 72 us (0.77)
  Pallas kernels: 84.5 us -> 63.4 us
    pallas_call x1, Pallas kernels: 44.8 us -> 23.1 us  [on_device(): pl.pallas_call(functools.partial(head_kernel, rows, cols, n_lat), out_sha...]
where the time goes in v3:
time: 72 us; the launch traced here: 71.7 us
  Pallas kernels  63.4 us (88%)
  local copies, waits for them, and re-layouts  7.62 us (11%)
    pallas_call x1, Pallas kernels, on_device(): pl.pallas_call(functools.partial(head_kernel, rows, cols, n_lat), out_sha...  23.1 us
    pallas_call x1, Pallas kernels, on_device(): pl.pallas_call(functools.partial(gather_kernel, n_lat, n_lon, rows, cols)...  22.1 us
    pallas_call x1, Pallas kernels, on_device(): pl.pallas_call(functools.partial(scatter_kernel, n_lat, n_lon, rows, cols...  18.1 us
    unnamed x14, local copies, waits for them, and re-layouts  7.62 us

profile of v3, /device:TPU:0, one launch (start us, length us, event | category | flops | bytes accessed | tf_op | source)
XLA Modules:
  0.0 71.7 jit_solution(6841993158907387572)
XLA Ops:
  0.6 0.0 copy-start
  0.6 1.8 %copy-done = bf16[5,3,3,256,128]{4,3,2,1,0:T(8,128)(2,1)S(1)} copy-done((bf16[5,3,3,256,128]{4,3,2,1,0:T(8,128)(2,1)S(1)}, bf16[5,3,3,256,128]{4,3,2,1,0:T(8,128)(2,1)}, u32[]{:S(2)}) %copy-start) | copy-done | bytes 2949144
  2.5 0.0 copy-start.1
  2.5 1.0 %copy-done.1 = bf16[24,64,128]{2,1,0:T(8,128)(2,1)S(1)} copy-done((bf16[24,64,128]{2,1,0:T(8,128)(2,1)S(1)}, bf16[24,64,128]{2,1,0:T(8,128)(2,1)}, u32[]{:S(2)}) %copy-start.1) | copy-done | bytes 393240
  3.5 0.0 copy-start.2
  3.5 1.0 %copy-done.2 = bf16[24,64,128]{2,1,0:T(8,128)(2,1)S(1)} copy-done((bf16[24,64,128]{2,1,0:T(8,128)(2,1)S(1)}, bf16[24,64,128]{2,1,0:T(8,128)(2,1)}, u32[]{:S(2)}) %copy-start.2) | copy-done | bytes 393240
  4.5 0.0 copy-start.3
  4.5 1.0 %copy-done.3 = bf16[5,128,256]{2,1,0:T(8,128)(2,1)S(1)} copy-done((bf16[5,128,256]{2,1,0:T(8,128)(2,1)S(1)}, bf16[5,128,256]{2,1,0:T(8,128)(2,1)}, u32[]{:S(2)}) %copy-start.3) | copy-done | bytes 327704
  5.4 0.0 copy-start.4
  5.4 0.7 copy-done.4
  6.1 22.1 %gather_halo.1 = (bf16[2,21,64,128]{3,2,1,0:T(8,128)(2,1)S(1)}, bf16[2,21,64,128]{3,2,1,0:T(8,128)(2,1)S(1)}, bf16[2,512,128]{2,1,0:T(8,128)(2,1)S(1)}, bf16[2,5...) custom-call(bf16[24,64,128]{2,1,0:T(8,128)(2,1)S(1)} %copy-done.1, ...), custom_call_target="tpu_custom_call" | custom-call | tf_op jit(solution)/shard_map/gather_halo/pallas_call | solution.py:396
  28.3 0.0 copy-start.5
  28.3 0.6 copy-done.5
  28.9 23.1 %head.1 = (bf16[2,24,64,128]{3,2,1,0:T(8,128)(2,1)S(1)}, bf16[2,24,64,128]{3,2,1,0:T(8,128)(2,1)S(1)}, bf16[2,21,64,128]{3,2,1,0:T(8,128)(2,1)S(1)}, bf16[2,21,6...) custom-call(s32[5]{0:T(128)S(1)} %copy-done.5, ...), custom_call_target="tpu_custom_call" | custom-call | tf_op jit(solution)/shard_map/head/pallas_call | solution.py:423
  52.0 18.1 %scatter_halo.1 = (bf16[24,64,128]{2,1,0:T(8,128)(2,1)S(1)}, bf16[24,64,128]{2,1,0:T(8,128)(2,1)S(1)}) custom-call(bf16[2,24,64,128]{3,2,1,0:T(8,128)(2,1)S(1)} %get-tuple-element.38.m_part, bf16[2,24,64,128]{3,2,1,0:T(8,128)(2,1)S(1)} %get-tuple-element.39.c_part, bf16[2,21,64,128]{3,2,1,0:T(8,128)(2,1)S(1)} %get-tuple-element.40.refs_0_, ...), custom_call_target="tpu_custom_call" | custom-call | tf_op jit(solution)/shard_map/scatter_halo/pallas_call | solution.py:452
  70.2 0.7 %copy.10 = bf16[24,64,128]{2,1,0:T(8,128)(2,1)} copy(bf16[24,64,128]{2,1,0:T(8,128)(2,1)S(1)} %get-tuple-element.50) | data formatting | bytes 786432
  70.9 0.7 %copy.11 = bf16[24,64,128]{2,1,0:T(8,128)(2,1)} copy(bf16[24,64,128]{2,1,0:T(8,128)(2,1)S(1)} %get-tuple-element.51) | data formatting | bytes 786432
Async XLA Ops:
  0.6 1.8 %copy-start = (bf16[5,3,3,256,128]{4,3,2,1,0:T(8,128)(2,1)S(1)}, bf16[5,3,3,256,128]{4,3,2,1,0:T(8,128)(2,1)}, u32[]{:S(2)}) copy-start(bf16[5,3,3,256,128]{4,3,2,1,0:T(8,128)(2,1)} %refs_2_.1) | copy-start | bytes 8847364
  2.5 1.0 %copy-start.1 = (bf16[24,64,128]{2,1,0:T(8,128)(2,1)S(1)}, bf16[24,64,128]{2,1,0:T(8,128)(2,1)}, u32[]{:S(2)}) copy-start(bf16[24,64,128]{2,1,0:T(8,128)(2,1)} %refs_0_.1) | copy-start | bytes 1179652
  3.5 1.0 %copy-start.2 = (bf16[24,64,128]{2,1,0:T(8,128)(2,1)S(1)}, bf16[24,64,128]{2,1,0:T(8,128)(2,1)}, u32[]{:S(2)}) copy-start(bf16[24,64,128]{2,1,0:T(8,128)(2,1)} %refs_1_.1) | copy-start | bytes 1179652
  4.5 1.0 %copy-start.3 = (bf16[5,128,256]{2,1,0:T(8,128)(2,1)S(1)}, bf16[5,128,256]{2,1,0:T(8,128)(2,1)}, u32[]{:S(2)}) copy-start(bf16[5,128,256]{2,1,0:T(8,128)(2,1)} %refs_3_.1) | copy-start | bytes 983044
  5.4 0.7 copy-start.4
  28.3 0.7 copy-start.5

commit v4 on v3

--- a/solution.py
+++ b/solution.py
@@ -392,7 +392,10 @@
 
     tile = jax.ShapeDtypeStruct((2, rows, cols, lanes), bf16)
     piece_pairs = [jax.ShapeDtypeStruct((2,) + piece(k), bf16) for k in range(8)]
-    own = (features, cotangent, branch_weight, merge_weight, branch_bias)
+    own = tuple(
+        pltpu.with_memory_space_constraint(a, pltpu.HBM)
+        for a in (features, cotangent, branch_weight, merge_weight, branch_bias)
+    )
     gathered = pl.pallas_call(
         functools.partial(gather_kernel, n_lat, n_lon, rows, cols),
         out_shape=piece_pairs + [jax.ShapeDtypeStruct((2,) + a.shape, a.dtype) for a in own],
@@ -438,7 +441,7 @@
         compiler_params=pltpu.CompilerParams(vmem_limit_bytes=32 * 2**20),
         name="head",
     )(
-        dilation_rates,
+        pltpu.with_memory_space_constraint(dilation_rates, pltpu.HBM),
         weights,
         biases,
         merges,

time: 72 us -> 65 us (0.903)
  local copies, waits for them, and re-layouts: 7.62 us -> 1.49 us
    unnamed x14 -> x2, local copies, waits for them, and re-layouts: 7.62 us -> 1.49 us
    pallas_call x1, Pallas kernels: 22.1 us -> 21.4 us  [on_device(): pl.pallas_call(functools.partial(gather_kernel, n_lat, n_lon, rows, cols)...]
where the time goes in v4:
time: 65 us; the launch traced here: 64.8 us
  Pallas kernels  62.7 us (96%)
  local copies, waits for them, and re-layouts  1.49 us (2%)
  between operations  0.66 us (1%)
    pallas_call x1, Pallas kernels, on_device(): pl.pallas_call(functools.partial(head_kernel, rows, cols, n_lat), out_sha...  23.2 us
    pallas_call x1, Pallas kernels, on_device(): pl.pallas_call(functools.partial(gather_kernel, n_lat, n_lon, rows, cols)...  21.4 us
    pallas_call x1, Pallas kernels, on_device(): pl.pallas_call(functools.partial(scatter_kernel, n_lat, n_lon, rows, cols...  18.1 us
    unnamed x2, local copies, waits for them, and re-layouts  1.49 us

profile of v4, /device:TPU:0, one launch (start us, length us, event | category | flops | bytes accessed | tf_op | source)
XLA Modules:
  0.0 64.8 jit_solution(937553749210040916)
XLA Ops:
  0.6 21.4 %gather_halo.1 = (bf16[2,21,64,128]{3,2,1,0:T(8,128)(2,1)S(1)}, bf16[2,21,64,128]{3,2,1,0:T(8,128)(2,1)S(1)}, bf16[2,512,128]{2,1,0:T(8,128)(2,1)S(1)}, bf16[2,5...) custom-call(bf16[24,64,128]{2,1,0:T(8,128)(2,1)} %refs_0_.1, ...), custom_call_target="tpu_custom_call" | custom-call | tf_op jit(solution)/shard_map/gather_halo/pallas_call | solution.py:399
  22.0 23.2 %head.1 = (bf16[2,24,64,128]{3,2,1,0:T(8,128)(2,1)S(1)}, bf16[2,24,64,128]{3,2,1,0:T(8,128)(2,1)S(1)}, bf16[2,21,64,128]{3,2,1,0:T(8,128)(2,1)S(1)}, bf16[2,21,6...) custom-call(s32[5]{0:T(128)} %info.1, ...), custom_call_target="tpu_custom_call" | custom-call | tf_op jit(solution)/shard_map/head/pallas_call | solution.py:426
  45.2 18.1 %scatter_halo.1 = (bf16[24,64,128]{2,1,0:T(8,128)(2,1)S(1)}, bf16[24,64,128]{2,1,0:T(8,128)(2,1)S(1)}) custom-call(bf16[2,24,64,128]{3,2,1,0:T(8,128)(2,1)S(1)} %get-tuple-element.38.m_part, bf16[2,24,64,128]{3,2,1,0:T(8,128)(2,1)S(1)} %get-tuple-element.39.c_part, bf16[2,21,64,128]{3,2,1,0:T(8,128)(2,1)S(1)} %get-tuple-element.40.refs_0_, ...), custom_call_target="tpu_custom_call" | custom-call | tf_op jit(solution)/shard_map/scatter_halo/pallas_call | solution.py:455
  63.4 0.7 %copy.10 = bf16[24,64,128]{2,1,0:T(8,128)(2,1)} copy(bf16[24,64,128]{2,1,0:T(8,128)(2,1)S(1)} %get-tuple-element.50) | data formatting | bytes 786432
  64.1 0.7 %copy.11 = bf16[24,64,128]{2,1,0:T(8,128)(2,1)} copy(bf16[24,64,128]{2,1,0:T(8,128)(2,1)S(1)} %get-tuple-element.51) | data formatting | bytes 786432

commit v5 on v4

--- a/solution.py
+++ b/solution.py
@@ -254,8 +254,7 @@
     sigma = 1.0 / (1.0 + jnp.exp(-preact))
     activated = (preact * sigma).astype(jnp.bfloat16)
     project = jnp.concatenate([merge[h, b] for h in range(2)], axis=0)
-    here = pl.ds(pl.multiple_of(first_row * cols, cells), cells)
-    merged[here, :] += jnp.dot(activated, project, preferred_element_type=jnp.float32)
+    merged[...] += jnp.dot(activated, project, preferred_element_type=jnp.float32)
     own_cot = jnp.concatenate(
         [cot[c, pl.ds(first_row, own_rows)].reshape(cells, LANES) for c in range(2)], axis=1
     )
@@ -284,7 +283,7 @@
             m_out[c] = (
                 merged[:, c * LANES : (c + 1) * LANES]
                 .astype(jnp.bfloat16)
-                .reshape(rows, cols, LANES)
+                .reshape(rows // 2, cols, LANES)
             )
             c_out[c] = total[c, RMAX : RMAX + rows, PADL:right_col, :].astype(jnp.bfloat16)
             for k in range(8):
@@ -311,7 +310,7 @@
     from_sib = refs[10:18]
     staged = refs[18:26]
     landed = refs[26:34]
-    m_sib, c_sib, acc, strip, send, recv, send2, recv2 = refs[34:]
+    c_sib, acc, strip, send, recv, send2, recv2 = refs[34:]
     at = Where(n_lat, n_lon)
     me = at.ch
     at.barrier()
@@ -332,7 +331,10 @@
     for k in order:
         at.when(k, lambda k=k: to_sibling(parts[k], from_sib[k], k).start())
     to_sibling(c_part, c_sib, 8).start()
-    to_sibling(m_part, m_sib, 9).start()
+    own_rows = pl.ds(me * (rows // 2), rows // 2)
+    their_rows = pl.ds((1 - me) * (rows // 2), rows // 2)
+    to_sibling(m_part, m_out.at[own_rows], 9).start()
+    m_out[own_rows] = m_part[me]
 
     def reduce_and_send(k):
         to_sibling(parts[k], from_sib[k], k).wait()
@@ -346,10 +348,8 @@
 
     to_sibling(c_part, c_sib, 8).wait()
     acc[...] = c_part[me].astype(jnp.float32) + c_sib[...].astype(jnp.float32)
-    to_sibling(m_part, m_sib, 9).wait()
-    m_out[...] = (m_part[me].astype(jnp.float32) + m_sib[...].astype(jnp.float32)).astype(
-        jnp.bfloat16
-    )
+    to_sibling(m_part, m_out.at[own_rows], 9).wait_send()
+    to_sibling(m_part, m_out.at[their_rows], 9).wait_recv()
 
     def arrive(k):
         dlat, dlon = SIDES[k]
@@ -422,7 +422,7 @@
     pad_cols = PADL + cols + 24
     padded_shape = (2, rows + 2 * RMAX, pad_cols, lanes)
 
-    outs = [tile, tile] + piece_pairs
+    outs = [jax.ShapeDtypeStruct((2, rows // 2, cols, lanes), bf16), tile] + piece_pairs
     head = pl.pallas_call(
         functools.partial(head_kernel, rows, cols, n_lat),
         out_shape=outs,
@@ -434,7 +434,7 @@
             scratch_shapes=[
                 pltpu.VMEM(padded_shape, f32),
                 pltpu.VMEM(padded_shape, f32),
-                pltpu.VMEM((rows * cols, channels), f32),
+                pltpu.VMEM((rows // 2 * cols, channels), f32),
                 pltpu.VMEM((flat, lanes), f32),
             ],
         ),
@@ -461,7 +461,6 @@
         + single
         + single
         + [
-            pltpu.VMEM((rows, cols, lanes), bf16),
             pltpu.VMEM((rows, cols, lanes), bf16),
             pltpu.VMEM((rows, cols, lanes), f32),
             pltpu.VMEM((2, flat, lanes), f32),

time: 65 us -> 64.9 us (level)
  no operation moved by 1% of the time
where the time goes in v5:
time: 64.9 us; the launch traced here: 64.7 us
  Pallas kernels  62.6 us (96%)
  local copies, waits for them, and re-layouts  1.49 us (2%)
  between operations  0.66 us (1%)
    pallas_call x1, Pallas kernels, on_device(): pl.pallas_call(functools.partial(head_kernel, rows, cols, n_lat), out_sha...  23.1 us
    pallas_call x1, Pallas kernels, on_device(): pl.pallas_call(functools.partial(gather_kernel, n_lat, n_lon, rows, cols)...  21.4 us
    pallas_call x1, Pallas kernels, on_device(): pl.pallas_call(functools.partial(scatter_kernel, n_lat, n_lon, rows, cols...  18.1 us
    unnamed x2, local copies, waits for them, and re-layouts  1.49 us

profile of v5, /device:TPU:0, one launch (start us, length us, event | category | flops | bytes accessed | tf_op | source)
XLA Modules:
  0.0 64.7 jit_solution(100488749109124414)
XLA Ops:
  0.6 21.4 %gather_halo.1 = (bf16[2,21,64,128]{3,2,1,0:T(8,128)(2,1)S(1)}, bf16[2,21,64,128]{3,2,1,0:T(8,128)(2,1)S(1)}, bf16[2,512,128]{2,1,0:T(8,128)(2,1)S(1)}, bf16[2,5...) custom-call(bf16[24,64,128]{2,1,0:T(8,128)(2,1)} %refs_0_.1, ...), custom_call_target="tpu_custom_call" | custom-call | tf_op jit(solution)/shard_map/gather_halo/pallas_call | solution.py:399
  22.0 23.1 %head.1 = (bf16[2,12,64,128]{3,2,1,0:T(8,128)(2,1)S(1)}, bf16[2,24,64,128]{3,2,1,0:T(8,128)(2,1)S(1)}, bf16[2,21,64,128]{3,2,1,0:T(8,128)(2,1)S(1)}, bf16[2,21,6...) custom-call(s32[5]{0:T(128)} %info.1, ...), custom_call_target="tpu_custom_call" | custom-call | tf_op jit(solution)/shard_map/head/pallas_call | solution.py:426
  45.1 18.1 %scatter_halo.1 = (bf16[24,64,128]{2,1,0:T(8,128)(2,1)S(1)}, bf16[24,64,128]{2,1,0:T(8,128)(2,1)S(1)}) custom-call(bf16[2,12,64,128]{3,2,1,0:T(8,128)(2,1)S(1)} %get-tuple-element.38.m_part, bf16[2,24,64,128]{3,2,1,0:T(8,128)(2,1)S(1)} %get-tuple-element.39.c_part, bf16[2,21,64,128]{3,2,1,0:T(8,128)(2,1)S(1)} %get-tuple-element.40.refs_0_, ...), custom_call_target="tpu_custom_call" | custom-call | tf_op jit(solution)/shard_map/scatter_halo/pallas_call | solution.py:455
  63.2 0.7 %copy.10 = bf16[24,64,128]{2,1,0:T(8,128)(2,1)} copy(bf16[24,64,128]{2,1,0:T(8,128)(2,1)S(1)} %get-tuple-element.50) | data formatting | bytes 786432
  64.0 0.7 %copy.11 = bf16[24,64,128]{2,1,0:T(8,128)(2,1)} copy(bf16[24,64,128]{2,1,0:T(8,128)(2,1)S(1)} %get-tuple-element.51) | data formatting | bytes 786432
